TPU v7x, 32 devices: a whole 2x2x4 slice. The times are simulated.
32 devices in a mesh: dp: 2 (over y), expert: 16 (over z, x, core).
Axes of the slice: x: 2, y: 2, z: 4, core: 2. Of those that a mesh axis runs over, the one named last changes fastest.
Arguments:
- tokens: bfloat16 [4096, 3584], P(('dp', 'expert')), may hold values from -6 to 6
- out_cotangent: bfloat16 [4096, 3584], P(('dp', 'expert')), may hold values from -6 to 6
- expert_ids: int32 [4096, 8], P(('dp', 'expert')), may hold values from 0 to 255, as said below
- gate_fixed: int32 [4096, 8], P(('dp', 'expert')), may hold values from 4096 to 65535
- w_gate: bfloat16 [16, 3584, 128], P('expert', 'dp'), may hold values from -0.09375 to 0.09375
- w_up: bfloat16 [16, 3584, 128], P('expert', 'dp'), may hold values from -0.09375 to 0.09375
- w_down: bfloat16 [16, 3584, 128], P('expert', 'dp'), may hold values from -0.125 to 0.125
Outputs:
- layer_out: bfloat16 [4096, 3584], P(('dp', 'expert'))
- token_grad: bfloat16 [4096, 3584], P(('dp', 'expert'))
- grad_gate: float32 [16, 3584, 128], P('expert', 'dp')
- grad_up: float32 [16, 3584, 128], P('expert', 'dp')
- grad_down: float32 [16, 3584, 128], P('expert', 'dp')
Inputs may be any that keep to these rules, and one draw needn't show every extreme that they name: `expert_ids`: each row names 8 different experts. Within the 128 rows of one device each expert below 1 is named by 1 to 4 rows; in every draw one expert below 1 is named by exactly 4 rows on every device.
All inputs are finite; a program needn't handle non-finite values.
Results may differ from a plain program's by a relative error of at most 0.014.
Values may be sent and summed in bfloat16 or wider, within the bound.
A program may use at most 128 MiB of HBM per device.

v0:
```python
import jax
import jax.numpy as jnp
from jax import lax
from jax.sharding import PartitionSpec as P

SPLIT = 16
CAP = 4


SCALE = 2.0 ** (-16)
HIGH = lax.Precision.HIGHEST


def routing(ids, gates, window, capacity):
    wanted = jnp.arange(window, dtype=jnp.int32)
    hits = ids[:, :, None] == wanted[None, None, :]
    member = jnp.any(hits, axis=1)
    weight = jnp.sum(jnp.where(hits, gates[:, :, None], 0), axis=1).astype(jnp.float32) * SCALE
    rank = jnp.cumsum(member.astype(jnp.int32), axis=0) - 1
    slots = jnp.arange(capacity, dtype=jnp.int32)
    pick = jnp.logical_and(member[:, :, None], rank[:, :, None] == slots[None, None, :])
    select = jnp.where(pick, 1.0, 0.0).astype(jnp.float32)
    slot_gate = jnp.sum(select * weight[:, :, None], axis=0)
    return (select, slot_gate)


def expert_math(inputs, cotangents, gate_w, up_w, down_w):
    gate_pre = jnp.einsum("prf,pfh->rh", inputs, gate_w, preferred_element_type=jnp.float32)
    up_pre = jnp.einsum("prf,pfh->rh", inputs, up_w, preferred_element_type=jnp.float32)
    sig = jax.nn.sigmoid(gate_pre)
    act = gate_pre * sig
    hidden = (act * up_pre).astype(jnp.bfloat16)
    partial_out = jnp.einsum("rh,pfh->prf", hidden, down_w, preferred_element_type=jnp.float32)
    d_hidden = jnp.einsum("prf,pfh->rh", cotangents, down_w, preferred_element_type=jnp.float32)
    d_gate = (d_hidden * up_pre * sig * (1.0 + gate_pre * (1.0 - sig))).astype(jnp.bfloat16)
    d_up = (d_hidden * act).astype(jnp.bfloat16)
    partial_grad = jnp.einsum(
        "rh,pfh->prf", d_gate, gate_w, preferred_element_type=jnp.float32
    ) + jnp.einsum("rh,pfh->prf", d_up, up_w, preferred_element_type=jnp.float32)
    term = jnp.concatenate(
        [
            jnp.einsum("prf,rh->pfh", inputs, d_gate, preferred_element_type=jnp.float32),
            jnp.einsum("prf,rh->pfh", inputs, d_up, preferred_element_type=jnp.float32),
            jnp.einsum("prf,rh->pfh", cotangents, hidden, preferred_element_type=jnp.float32),
        ],
        axis=2,
    )
    return (partial_out, partial_grad, term.reshape(-1, term.shape[2]))


def per_device(tokens, out_cotangent, expert_ids, gate_fixed, w_gate, w_up, w_down):
    tok_rows, width = tokens.shape
    groups = lax.axis_size("expert")
    window = groups // SPLIT
    hid = w_gate.shape[2]
    parts = 1
    feat = width // parts
    select, slot_gate = routing(expert_ids, gate_fixed, window, CAP)
    select_b = select.astype(jnp.bfloat16)
    tok3 = tokens.reshape(tok_rows, parts, feat)
    cot3 = out_cotangent.reshape(tok_rows, parts, feat)
    slot_tokens = jnp.einsum(
        "tec,tsf->escf", select_b, tok3, preferred_element_type=jnp.float32
    ).astype(jnp.bfloat16)
    picked = jnp.einsum("tec,tsf->escf", select_b, cot3, preferred_element_type=jnp.float32)
    slot_cot = (picked * slot_gate[:, None, :, None]).astype(jnp.bfloat16)
    payload = jnp.stack([slot_tokens, slot_cot], axis=2)
    gate_full, up_full, down_full = (
        lax.all_gather(w_gate, "dp", axis=1, tiled=True),
        lax.all_gather(w_up, "dp", axis=1, tiled=True),
        lax.all_gather(w_down, "dp", axis=1, tiled=True),
    )
    outgoing = jnp.broadcast_to(payload, (window, SPLIT, 2, CAP, width)).reshape(
        groups, 2, CAP, width
    )
    arrived = lax.all_to_all(outgoing, "expert", split_axis=0, concat_axis=0, tiled=True)
    pieces = arrived[None]
    inputs = pieces[:, :, 0].reshape(parts, groups * CAP, feat)
    cotangents = pieces[:, :, 1].reshape(parts, groups * CAP, feat)
    partial_out, partial_grad, term = expert_math(inputs, cotangents, gate_full, up_full, down_full)
    summed = lax.psum_scatter(
        term.astype(jnp.bfloat16), "dp", scatter_dimension=0, tiled=True
    ).astype(jnp.float32)
    grad_gate = summed[:, :hid][None]
    grad_up = summed[:, hid : 2 * hid][None]
    grad_down = summed[:, 2 * hid :][None]
    results = jnp.stack(
        [
            partial_out.reshape(parts, groups, CAP, feat),
            partial_grad.reshape(parts, groups, CAP, feat),
        ],
        axis=2,
    )
    returned = lax.all_to_all(
        results[0].astype(jnp.bfloat16), "expert", split_axis=0, concat_axis=0, tiled=True
    ).astype(jnp.float32)
    combined = jnp.sum(
        returned.reshape(window, SPLIT, 2, CAP, width), axis=1, keepdims=True
    ).astype(jnp.bfloat16)
    weighted = select * slot_gate[None, :, :]
    layer_out = jnp.einsum(
        "tec,ehcf->thf", weighted, combined[:, :, 0].astype(jnp.float32), precision=HIGH
    )
    token_grad = jnp.einsum(
        "tec,ehcf->thf", select, combined[:, :, 1].astype(jnp.float32), precision=HIGH
    )
    return (
        layer_out.reshape(tok_rows, width).astype(jnp.bfloat16),
        token_grad.reshape(tok_rows, width).astype(jnp.bfloat16),
        grad_gate,
        grad_up,
        grad_down,
    )


def solution(mesh):
    return jax.shard_map(
        per_device,
        mesh=mesh,
        in_specs=(
            P(("dp", "expert"), None),
            P(("dp", "expert"), None),
            P(("dp", "expert"), None),
            P(("dp", "expert"), None),
            P("expert", "dp", None),
            P("expert", "dp", None),
            P("expert", "dp", None),
        ),
        out_specs=(
            P(("dp", "expert"), None),
            P(("dp", "expert"), None),
            P("expert", "dp", None),
            P("expert", "dp", None),
            P("expert", "dp", None),
        ),
        check_vma=False,
    )
```

profile of v0, /device:TPU:0, one launch (start us, length us, event | category | flops | bytes accessed | tf_op | source)
XLA Modules:
  0.0 122.6 jit_solution(11350269692706062275)
XLA Ops:
  7.2 0.0 copy-start
  7.2 0.0 copy-start.2
  7.2 0.8 fusion.35
  8.0 0.7 select_reduce_fusion
  8.7 0.1 copy.26
  8.8 0.2 reduce-window.7
  9.0 0.1 add_reduce_fusion
  9.1 0.1 multiply_reduce_fusion
  9.2 0.0 copy-done
  9.2 0.3 fusion.8
  9.6 0.0 copy-start.3
  9.6 1.6 %fusion.9 = bf16[1,1,1,4,3584]{4,3,2,1,0:T(4,128)(2,1)S(1)} fusion(bf16[128,3584]{1,0:T(8,128)(2,1)} %param.8, s32[128]{0:T(128)S(1)} %add_reduce_fusion, pred[128]{0:T(512)(128)(4,1)S(1)} %get-tuple-element.25, f32[4]{0:T(128)S(1)} %multiply_reduce_fusion), kind=kOutput, calls=%fused_computation.18 | convolution fusion | flops 3700736 | bytes 946832 | tf_op jit(solution)/shard_map/tec,tsf->escf/dot_general | solution.py:65
  11.2 0.1 maximum_bitcast_fusion.2
  11.2 1.2 reshape.402
  12.4 7.4 %all-to-all-start = ((bf16[16,2,4,3584]{3,2,1,0:T(4,128)(2,1)}), bf16[16,2,4,3584]{3,2,1,0:T(4,128)(2,1)}, u32[]{:S(2)}, u32[]{:S(2)}) async-start(bf16[16,2,4,3584]{3,2,1,0:T(4,128)(2,1)} %reshape.402), calls=%async_computation | async-start | bytes 1835008 | tf_op jit(solution)/shard_map/all_to_all | solution.py:76
  19.8 0.0 reduce-scatter.2.cloned.1.call-start
  19.9 0.0 copy-done.2
  19.9 13.5 %all_gather.9 = bf16[1,3584,128]{2,1,0:T(8,128)(2,1)S(1)} all-gather(bf16[1,1792,128]{2,1,0:T(8,128)(2,1)S(1)} %copy-done.2), channel_id=1, replica_groups=mesh['dp'=2,'expert'=16] {'dp'}, dimensions={1}, use_global_device_ids=true | all-gather | bytes 1376256 | tf_op jit(solution)/shard_map/all_gather | solution.py:69
  33.3 0.0 copy-done.3
  33.3 12.8 %all_gather.10 = bf16[1,3584,128]{2,1,0:T(8,128)(2,1)S(1)} all-gather(bf16[1,1792,128]{2,1,0:T(8,128)(2,1)S(1)} %copy-done.3), channel_id=1, replica_groups=mesh['dp'=2,'expert'=16] {'dp'}, dimensions={1}, use_global_device_ids=true | all-gather | bytes 1376256 | tf_op jit(solution)/shard_map/all_gather | solution.py:70
  46.1 13.7 %all_gather.11 = bf16[1,3584,128]{2,1,0:T(8,128)(2,1)} all-gather(bf16[1,1792,128]{2,1,0:T(8,128)(2,1)} %param.13), channel_id=1, replica_groups=mesh['dp'=2,'expert'=16] {'dp'}, dimensions={1}, use_global_device_ids=true | all-gather | bytes 1376256 | tf_op jit(solution)/shard_map/all_gather | solution.py:71
  59.8 0.0 all-to-all-done
  59.8 2.2 %fusion.36 = (bf16[1,16,1,4,3584]{4,3,2,1,0:T(4,128)(2,1)S(1)}, bf16[1,16,1,4,3584]{4,3,2,1,0:T(4,128)(2,1)}) fusion(bf16[1,16,2,4,3584]{4,3,2,1,0:T(4,128)(2,1)} %bitcast.11), kind=kLoop, calls=%fused_computation.68 | loop fusion | bytes 1835008 | tf_op jit(solution)/shard_map/slice | solution.py:79
  62.0 0.9 reshape.407
  62.9 1.1 reshape.403
  64.0 0.0 copy-start.1
  64.0 0.3 fusion.18
  64.3 1.6 %fusion.10 = f32[64,128]{1,0:T(8,128)S(1)} fusion(bf16[64,3584]{1,0:T(8,128)(2,1)} %reshape.407, bf16[1,3584,128]{2,1,0:T(8,128)(2,1)} %all_gather.11), kind=kOutput, calls=%fused_computation.24 | convolution fusion | flops 58720256 | bytes 1409024 | tf_op jit(solution)/shard_map/prf,pfh->rh/dot_general | solution.py:34
  66.0 0.3 multiply_convert_fusion.2
  66.3 0.0 copy-done.1
  66.3 0.4 fusion.2
  66.8 0.4 fusion.1
  67.2 0.4 fusion
  67.6 1.7 %maximum_bitcast_fusion = bf16[3584,384]{0,1:T(8,128)(2,1)} fusion(bf16[1,3584,128]{1,2,0:T(8,128)(2,1)S(1)} %fusion.2, bf16[1,3584,128]{1,2,0:T(8,128)(2,1)S(1)} %fusion.1, bf16[1,3584,128]{1,2,0:T(8,128)(2,1)S(1)} %fusion), kind=kLoop, calls=%fused_computation.19 | loop fusion | flops 8257536 | bytes 5505024 | tf_op jit(solution)/shard_map/convert_element_type | solution.py:82
  69.4 0.0 reduce-scatter.2.cloned.1.call-update
  69.4 2.4 %fusion.5 = bf16[1,64,3584]{2,1,0:T(8,128)(2,1)} fusion(bf16[64,128]{1,0:T(8,128)(2,1)S(1)} %get-tuple-element.32, bf16[1,3584,128]{2,1,0:T(8,128)(2,1)} %all_gather.11), kind=kOutput, calls=%fused_computation.12 | convolution fusion | flops 58949632 | bytes 1392640 | tf_op jit(solution)/shard_map/rh,pfh->prf/dot_general | solution.py:33
  71.8 1.1 stack_reshape.8
  72.9 0.4 fusion.16
  73.4 0.4 fusion.4
  73.8 0.1 stack_reshape.9
  73.9 1.5 %maximum_bitcast_fusion.1 = bf16[16,2,4,3584]{3,2,1,0:T(4,128)(2,1)} fusion(bf16[1,16,1,4,3584]{4,3,2,1,0:T(4,128)(2,1)S(1)} %bitcast.100, bf16[1,16,1,4,3584]{4,3,2,1,0:T(4,128)(2,1)S(1)} %bitcast.99), kind=kLoop, calls=%fused_computation.23 | loop fusion | flops 458752 | bytes 1835008 | tf_op jit(solution)/shard_map/convert_element_type | solution.py:95
  75.5 5.3 %all-to-all-start.1 = ((bf16[16,2,4,3584]{3,2,1,0:T(4,128)(2,1)}), bf16[16,2,4,3584]{3,2,1,0:T(4,128)(2,1)S(1)}, u32[]{:S(2)}, u32[]{:S(2)}) async-start(bf16[16,2,4,3584]{3,2,1,0:T(4,128)(2,1)} %maximum_bitcast_fusion.1), calls=%async_computation.1 | async-start | bytes 1835008 | tf_op jit(solution)/shard_map/all_to_all | solution.py:94
  80.7 0.3 and_select_fusion
  81.1 20.5 %all-to-all-done.1 = bf16[16,2,4,3584]{3,2,1,0:T(4,128)(2,1)S(1)} async-done(((bf16[16,2,4,3584]{3,2,1,0:T(4,128)(2,1)}), bf16[16,2,4,3584]{3,2,1,0:T(4,128)(2,1)S(1)}, u32[]{:S(2)}, u32[]{:S(2)}) %all-to-all-start.1) | async-done | bytes 917536 | tf_op jit(solution)/shard_map/all_to_all | solution.py:94
  101.5 0.4 reduce_sum.32
  101.9 1.8 %convolution_convert_fusion.3 = bf16[128,3584]{1,0:T(8,128)(2,1)} fusion(f32[128,4]{1,0:T(8,128)S(1)} %bitcast.102, bf16[1,1,2,4,3584]{4,3,2,1,0:T(4,128)(2,1)S(1)} %bitcast.103), kind=kOutput, calls=%fused_computation.3 | convolution fusion | flops 22478848 | bytes 1011712 | tf_op jit(solution)/shard_map/tec,ehcf->thf/dot_general | solution.py:104
  103.7 1.8 %convolution_convert_fusion.4 = bf16[128,3584]{1,0:T(8,128)(2,1)} fusion(f32[128,4]{1,0:T(8,128)S(1)} %bitcast.101, bf16[1,1,2,4,3584]{4,3,2,1,0:T(4,128)(2,1)S(1)} %bitcast.104), kind=kOutput, calls=%fused_computation.4 | convolution fusion | flops 22478848 | bytes 1011712 | tf_op jit(solution)/shard_map/tec,ehcf->thf/dot_general | solution.py:101
  105.5 2.7 %reduce-scatter.2.cloned.1.call-done = bf16[1792,384]{0,1:T(8,128)(2,1)} async-done(((bf16[3584,384]{0,1:T(8,128)(2,1)}), bf16[1792,384]{0,1:T(8,128)(2,1)}) %reduce-scatter.2.cloned.1.call-update) | async-done | bytes 1376272 | tf_op jit(solution)/shard_map/reduce_scatter | solution.py:81
  108.2 1.5 %convert_element_type.114 = f32[1792,384]{0,1:T(8,128)S(1)} convert(bf16[1792,384]{0,1:T(8,128)(2,1)} %reduce-scatter.2.cloned.1.call-done) | non-fusion elementwise | flops 688128 | bytes 4128768 | tf_op jit(solution)/shard_map/convert_element_type | solution.py:83
  109.8 1.2 slice_bitcast_fusion
  110.9 2.4 %copy.31 = f32[1,1792,128]{2,1,0:T(8,128)} copy(f32[1,1792,128]{1,2,0:T(8,128)} %get-tuple-element.27) | data formatting | bytes 1835008
  113.3 1.2 copy.30
  114.6 1.2 copy.29
  (2 shorter events, 0.0 us)
Async XLA Ops:
  7.2 2.1 %copy-start = (bf16[128,3584]{1,0:T(8,128)(2,1)S(1)}, bf16[128,3584]{1,0:T(8,128)(2,1)}, u32[]{:S(2)}) copy-start(bf16[128,3584]{1,0:T(8,128)(2,1)} %param.7) | copy-start | bytes 2752516
  7.2 12.7 %copy-start.2 = (bf16[1,1792,128]{2,1,0:T(8,128)(2,1)S(1)}, bf16[1,1792,128]{2,1,0:T(8,128)(2,1)}, u32[]{:S(2)}) copy-start(bf16[1,1792,128]{2,1,0:T(8,128)(2,1)} %param.11) | copy-start | bytes 1376260
  9.6 23.7 %copy-start.3 = (bf16[1,1792,128]{2,1,0:T(8,128)(2,1)S(1)}, bf16[1,1792,128]{2,1,0:T(8,128)(2,1)}, u32[]{:S(2)}) copy-start(bf16[1,1792,128]{2,1,0:T(8,128)(2,1)} %param.12) | copy-start | bytes 1376260
  12.4 47.4 %all-to-all-start = ((bf16[16,2,4,3584]{3,2,1,0:T(4,128)(2,1)}), bf16[16,2,4,3584]{3,2,1,0:T(4,128)(2,1)}, u32[]{:S(2)}, u32[]{:S(2)}) async-start(bf16[16,2,4,3584]{3,2,1,0:T(4,128)(2,1)} %reshape.402), calls=%async_computation | async-start | bytes 1835008 | tf_op jit(solution)/shard_map/all_to_all | solution.py:76
  19.8 88.4 %reduce-scatter.2.cloned.1.call-start = ((), (), s32[]{:S(2)}) async-start(), calls=%async_computation.3 | async-start | bytes 4128768 | tf_op jit(solution)/shard_map/reduce_scatter | solution.py:81
  64.0 2.3 %copy-start.1 = (bf16[64,3584]{1,0:T(8,128)(2,1)S(1)}, bf16[64,3584]{1,0:T(8,128)(2,1)}, u32[]{:S(2)}) copy-start(bf16[64,3584]{1,0:T(8,128)(2,1)} %reshape.407) | copy-start | bytes 1376260
  75.5 26.1 %all-to-all-start.1 = ((bf16[16,2,4,3584]{3,2,1,0:T(4,128)(2,1)}), bf16[16,2,4,3584]{3,2,1,0:T(4,128)(2,1)S(1)}, u32[]{:S(2)}, u32[]{:S(2)}) async-start(bf16[16,2,4,3584]{3,2,1,0:T(4,128)(2,1)} %maximum_bitcast_fusion.1), calls=%async_computation.1 | async-start | bytes 1835008 | tf_op jit(solution)/shard_map/all_to_all | solution.py:94
Sparse Core Ops, SparseCore 0:
  69.5 38.6 reduce-scatter.1
where the time goes:
time: 123 us
  blocking collectives  39.9 us (32%)
  waiting for transfers between devices  23.2 us (19%)
  between operations  14.2 us (12%)
  local copies, waits for them, and re-layouts  12.8 us (10%)
  starting transfers between devices  12.7 us (10%)
  matrix products  12.4 us (10%)
  other arithmetic  7.48 us (6%)
    all_to_all x1, waiting for transfers between devices, per_device(): lax.all_to_all(results[0].astype(jnp.bfloat16), 'expert', split_axis=0, c...  20.5 us
    all_gather x1, blocking collectives, per_device(): lax.all_gather(w_down, 'dp', axis=1, tiled=True)  13.7 us
    all_gather x1, blocking collectives, per_device(): lax.all_gather(w_gate, 'dp', axis=1, tiled=True)  13.5 us
    all_gather x1, blocking collectives, per_device(): lax.all_gather(w_up, 'dp', axis=1, tiled=True)  12.8 us
    all_to_all x1, starting transfers between devices, per_device(): lax.all_to_all(outgoing, 'expert', split_axis=0, concat_axis=0, tiled=True)  7.4 us
    all_to_all x1, starting transfers between devices, per_device(): lax.all_to_all(results[0].astype(jnp.bfloat16), 'expert', split_axis=0, c...  5.25 us
    unnamed x11, local copies, waits for them, and re-layouts  4.87 us
    reduce_scatter x1, waiting for transfers between devices, per_device(): lax.psum_scatter(term.astype(jnp.bfloat16), 'dp', scatter_dimension=0, ti...  2.73 us
  transfers between devices with their start and end apart: 3, of which 2 were waited for; matrix products, arithmetic and copies ran while one was open for 8% of the time, Pallas kernels for 0%

commit v1 on v0

--- a/solution.py
+++ b/solution.py
@@ -2,6 +2,8 @@
 import jax.numpy as jnp
 from jax import lax
 from jax.sharding import PartitionSpec as P
+from jax.experimental import pallas as pl
+from jax.experimental.pallas import tpu as pltpu
 
 SPLIT = 16
 CAP = 4
@@ -113,9 +115,300 @@
     )
 
 
+MESH = pl.DeviceIdType.MESH
+F32 = jnp.float32
+BF16 = jnp.bfloat16
+
+
+def row_ids(shape):
+    return lax.broadcasted_iota(jnp.int32, shape, 0)
+
+
+def fold(v):
+    half = v.shape[1] // 2
+    return jnp.concatenate([v[:, :half], v[:, half:]], axis=0)
+
+
+def unfold(v):
+    rows = v.shape[0] // 2
+    return jnp.concatenate([v[:rows], v[rows:]], axis=1)
+
+
+def exchange_kernel(
+    ids_ref, gates_ref, tok_hbm, cot_hbm, wg_hbm, wu_hbm, wd_hbm,
+    x_out, act_out, slot_out, sel_out,
+    tok_v, cot_v, w_v, gath, act_v, part, pex_s, pex_r, res, ra, sb, rb, sc, rc,
+    ys, yr, ys2, yr2, load_sem, send_sem, recv_sem,
+):
+    y = lax.axis_index("dp")
+    e = lax.axis_index("expert")
+    z, x, c = e // 4, (e // 2) % 2, e % 2
+
+    def dev(zz, xx, cc):
+        return zz * 4 + xx * 2 + cc
+
+    def pos(zz, xx, cc):
+        return cc * 8 + xx * 4 + zz
+
+    near = [z, z + 1 - 2 * (z % 2), (z + 2) % 4, 3 - z]
+    peer_y = (1 - y, e)
+    peer_c = (y, dev(z, x, 1 - c))
+    peer_x = (y, dev(z, 1 - x, c))
+    peer_z = [None] + [(y, dev(zz, x, c)) for zz in near[1:]]
+
+    started = []
+
+    def remote(src, dst, target):
+        n = len(started)
+        copy = pltpu.make_async_remote_copy(
+            src_ref=src, dst_ref=dst, send_sem=send_sem.at[n], recv_sem=recv_sem.at[n],
+            device_id=target, device_id_type=MESH,
+        )
+        copy.start()
+        started.append(copy)
+        return copy
+
+    loads = [
+        pltpu.make_async_copy(tok_hbm, tok_v, load_sem.at[0]),
+        pltpu.make_async_copy(cot_hbm, cot_v, load_sem.at[1]),
+        pltpu.make_async_copy(wg_hbm, w_v.at[:, 0:128], load_sem.at[2]),
+        pltpu.make_async_copy(wu_hbm, w_v.at[:, 128:256], load_sem.at[3]),
+        pltpu.make_async_copy(wd_hbm, w_v.at[:, 256:384], load_sem.at[4]),
+    ]
+    for load in loads:
+        load.start()
+    barrier = pltpu.get_barrier_semaphore()
+    greeted = [peer_y, peer_c, peer_x] + peer_z[1:]
+    for target in greeted:
+        pl.semaphore_signal(barrier, inc=1, device_id=target, device_id_type=MESH)
+
+    hits = ids_ref[...] == 0
+    member = jnp.sum(jnp.where(hits, 1.0, 0.0), axis=1, keepdims=True)
+    weight = jnp.sum(jnp.where(hits, gates_ref[...].astype(F32), 0.0), axis=1, keepdims=True) * SCALE
+    n_tok = member.shape[0]
+    square = (n_tok, n_tok)
+    lane = lax.broadcasted_iota(jnp.int32, square, 1)
+    earlier = jnp.where(lane < row_ids(square), 1.0, 0.0).astype(BF16)
+    spread = jnp.broadcast_to(member, square)
+    rank = jnp.dot(earlier, spread.astype(BF16), preferred_element_type=F32)
+    wanted = jnp.where(lane < 2 * CAP, lane % CAP, n_tok).astype(F32)
+    sel = jnp.where(jnp.logical_and(rank == wanted, spread > 0.5), 1.0, 0.0)
+    sel_out[...] = sel.astype(BF16)
+    sel_t = jnp.transpose(sel)[:8].astype(BF16)
+    gate8 = jnp.sum(jnp.transpose(sel * weight)[:8], axis=1, keepdims=True)
+
+    loads[0].wait()
+    tok8 = jnp.dot(sel_t, tok_v[...], preferred_element_type=F32)
+    loads[1].wait()
+    cot8 = jnp.dot(sel_t, cot_v[...], preferred_element_type=F32) * gate8
+    half = tok8.shape[1] // 2
+    low = row_ids((8, half)) < 4
+
+    def mine(v, flip=False):
+        first, second = v[:, :half], v[:, half:]
+        return jnp.where((y == 0) != flip, first, second)
+
+    ys[...] = fold(jnp.where(low, mine(tok8, True), mine(cot8, True))).astype(BF16)
+    pl.semaphore_wait(barrier, len(greeted))
+    swap = remote(ys, yr, peer_y)
+    own_tok, own_cot = mine(tok8), mine(cot8)
+    swap.wait_recv()
+    got = unfold(yr[...].astype(F32))
+    got_r = pltpu.roll(got, 4, 0)
+    own_rows = jnp.logical_xor(low, y != 0)
+    chunk = jnp.concatenate(
+        [
+            jnp.where(own_rows, own_tok, jnp.where(low, got, got_r)),
+            jnp.where(own_rows, own_cot, jnp.where(low, got_r, got)),
+        ],
+        axis=0,
+    )
+    here = pos(z, x, c)
+    gath[here] = chunk.astype(BF16)
+
+    over_z, over_x, over_c = [None], [], []
+    for k in (1, 2, 3):
+        over_z.append(remote(gath.at[here], gath.at[here], peer_z[k]))
+    for k in range(4):
+        at = pos(near[k], x, c)
+        if k:
+            over_z[k].wait_recv()
+        over_x.append(remote(gath.at[at], gath.at[at], peer_x))
+        over_c.append(remote(gath.at[at], gath.at[at], peer_c))
+    for k in range(4):
+        at = pos(near[k], 1 - x, c)
+        over_x[k].wait_recv()
+        over_c.append(remote(gath.at[at], gath.at[at], peer_c))
+
+    for load in loads[2:]:
+        load.wait()
+
+    def project(h):
+        rows = gath[pl.ds(h * 8, 8)].reshape(128, half)
+        p = jnp.dot(rows, w_v[...], preferred_element_type=F32).reshape(8, 16, 384)
+        both = jnp.concatenate([p[:, :8, :256], p[:, 8:, 256:]], axis=2).reshape(64, 384)
+        part[h] = both
+        pex_s[h] = both.astype(BF16)
+        return remote(pex_s.at[h], pex_r.at[h], peer_y)
+
+    def activate(h):
+        total = part[h] + pex_r[h].astype(F32)
+        gate_pre, up_pre, d_hidden = total[:, :128], total[:, 128:256], total[:, 256:]
+        sig = jax.nn.sigmoid(gate_pre)
+        act = gate_pre * sig
+        hidden = (act * up_pre).astype(BF16)
+        d_gate = (d_hidden * up_pre * sig * (1.0 + gate_pre * (1.0 - sig))).astype(BF16)
+        d_up = (d_hidden * act).astype(BF16)
+        d_both = jnp.concatenate([d_gate, d_up], axis=1)
+        nt = (((1,), (1,)), ((), ()))
+        out = lax.dot_general(hidden, w_v[:, 256:], nt, preferred_element_type=F32)
+        grad = lax.dot_general(d_both, w_v[:, :256], nt, preferred_element_type=F32)
+        res[pl.ds(h * 8, 8)] = jnp.concatenate(
+            [out.reshape(8, 8, half), grad.reshape(8, 8, half)], axis=1
+        ).astype(BF16)
+        top = jnp.concatenate([d_both.astype(F32).reshape(8, 8, 256), jnp.zeros((8, 8, 128), F32)], axis=2)
+        bottom = jnp.concatenate([jnp.zeros((8, 8, 256), F32), hidden.astype(F32).reshape(8, 8, 128)], axis=2)
+        act_v[pl.ds(h * 8, 8)] = jnp.concatenate([top, bottom], axis=1).astype(BF16)
+
+    swap_own = project(c)
+    for copy in over_c:
+        copy.wait_recv()
+    swap_other = project(1 - c)
+    keep_x = pltpu.make_async_copy(gath, x_out, load_sem.at[5])
+    keep_x.start()
+    swap_other.wait_recv()
+    activate(1 - c)
+    to_core = []
+    for xx in (1 - x, x):
+        src = res.at[pl.ds((1 - c) * 8 + xx * 4, 4)]
+        to_core.append(remote(src, ra.at[pl.ds(xx * 4, 4)], peer_c))
+    swap_own.wait_recv()
+    activate(c)
+    keep_act = pltpu.make_async_copy(act_v, act_out, load_sem.at[6])
+    keep_act.start()
+    to_core[0].wait_recv()
+    to_x = [None] * 4
+    for k in (3, 2, 1, 0):
+        zz = near[k]
+        sb[k] = (res[pos(zz, 1 - x, c)].astype(F32) + ra[(1 - x) * 4 + zz].astype(F32)).astype(BF16)
+        to_x[k] = remote(sb.at[k], rb.at[k], peer_x)
+    to_core[1].wait_recv()
+
+    def summed(k):
+        zz = near[k]
+        mid = res[pos(zz, x, c)].astype(F32) + ra[x * 4 + zz].astype(F32)
+        to_x[k].wait_recv()
+        return mid + rb[k].astype(F32)
+
+    to_z = [None] * 4
+    for k in (3, 2, 1):
+        sc[k] = summed(k).astype(BF16)
+        to_z[k] = remote(sc.at[k], rc.at[k], peer_z[k])
+    total = summed(0)
+    for k in (1, 2, 3):
+        to_z[k].wait_recv()
+        total = total + rc[k].astype(F32)
+    out8, grad8 = total[:8], total[8:]
+    for_0 = jnp.where(low, out8, pltpu.roll(grad8, 4, 0))
+    for_1 = jnp.where(low, pltpu.roll(out8, 4, 0), grad8)
+    ys2[...] = fold(jnp.where(y == 0, for_1, for_0)).astype(BF16)
+    swap = remote(ys2, yr2, peer_y)
+    mine8 = jnp.where(y == 0, for_0, for_1).astype(BF16).astype(F32)
+    scale = jnp.where(row_ids((8, 1)) < 4, gate8, 1.0)
+    swap.wait_recv()
+    got = unfold(yr2[...].astype(F32))
+    slot_out[:, :half] = jnp.where(y == 0, mine8, got) * scale
+    slot_out[:, half:] = jnp.where(y == 0, got, mine8) * scale
+    keep_x.wait()
+    keep_act.wait()
+    for copy in started:
+        copy.wait_send()
+
+
+def output_kernel(x_ref, act_ref, slot_ref, sel_ref, out_ref, tg_ref, gg_ref, gu_ref, gd_ref):
+    sel = sel_ref[...][:, :8].astype(F32)
+    lane = lax.broadcasted_iota(jnp.int32, sel.shape, 1)
+    slots = slot_ref[...].astype(BF16)
+    for ref, keep in ((out_ref, lane < 4), (tg_ref, lane >= 4)):
+        picks = jnp.where(keep, sel, 0.0).astype(BF16)
+        ref[...] = jnp.dot(picks, slots, preferred_element_type=F32).astype(BF16)
+    tn = (((0,), (0,)), ((), ()))
+    grads = lax.dot_general(x_ref[...], act_ref[...], tn, preferred_element_type=F32)
+    for n, ref in enumerate((gg_ref, gu_ref, gd_ref)):
+        ref[...] = grads[:, n * 128 : (n + 1) * 128]
+
+
+def per_device_fused(tokens, out_cotangent, expert_ids, gate_fixed, w_gate, w_up, w_down):
+    n_tok, width = tokens.shape
+    half = width // 2
+    hbm = pl.BlockSpec(memory_space=pl.ANY)
+    vmem = pl.BlockSpec(memory_space=pltpu.VMEM)
+    copies = 28
+    chunks = lambda n: pltpu.VMEM((n, 16, half), BF16)
+    x_all, act, slots, sel = pl.pallas_call(
+        exchange_kernel,
+        out_shape=(
+            jax.ShapeDtypeStruct((16, 16, half), BF16),
+            jax.ShapeDtypeStruct((16, 16, 384), BF16),
+            jax.ShapeDtypeStruct((8, width), F32),
+            jax.ShapeDtypeStruct((n_tok, n_tok), BF16),
+        ),
+        in_specs=[vmem] * 2 + [hbm] * 5,
+        out_specs=(hbm, hbm, vmem, vmem),
+        scratch_shapes=[
+            pltpu.VMEM((n_tok, width), BF16),
+            pltpu.VMEM((n_tok, width), BF16),
+            pltpu.VMEM((half, 384), BF16),
+            chunks(16),
+            pltpu.VMEM((16, 16, 384), BF16),
+            pltpu.VMEM((2, 64, 384), F32),
+            pltpu.VMEM((2, 64, 384), BF16),
+            pltpu.VMEM((2, 64, 384), BF16),
+            chunks(16),
+            chunks(8),
+            chunks(4),
+            chunks(4),
+            chunks(4),
+            chunks(4),
+        ]
+        + [pltpu.VMEM((16, half // 2), BF16)] * 4
+        + [
+            pltpu.SemaphoreType.DMA((7,)),
+            pltpu.SemaphoreType.DMA((copies,)),
+            pltpu.SemaphoreType.DMA((copies,)),
+        ],
+        compiler_params=pltpu.CompilerParams(
+            collective_id=0, has_side_effects=True, vmem_limit_bytes=40 * 1024 * 1024
+        ),
+        cost_estimate=pl.CostEstimate(flops=400_000_000, bytes_accessed=6_000_000, transcendentals=16384),
+        name="exchange",
+    )(expert_ids, gate_fixed, tokens, out_cotangent, w_gate[0], w_up[0], w_down[0])
+    steps = 2
+    grad_spec = pl.BlockSpec((half // steps, 128), lambda i: (i, 0))
+    tok_spec = pl.BlockSpec((n_tok, width // steps), lambda i: (0, i))
+    layer_out, token_grad, gg, gu, gd = pl.pallas_call(
+        output_kernel,
+        grid=(steps,),
+        out_shape=(jax.ShapeDtypeStruct((n_tok, width), BF16),) * 2
+        + (jax.ShapeDtypeStruct((half, 128), F32),) * 3,
+        in_specs=[
+            pl.BlockSpec((256, half // steps), lambda i: (0, i)),
+            pl.BlockSpec((256, 384), lambda i: (0, 0)),
+            pl.BlockSpec((8, width // steps), lambda i: (0, i)),
+            pl.BlockSpec((n_tok, n_tok), lambda i: (0, 0)),
+        ],
+        out_specs=(tok_spec, tok_spec, grad_spec, grad_spec, grad_spec),
+        compiler_params=pltpu.CompilerParams(vmem_limit_bytes=32 * 1024 * 1024),
+        cost_estimate=pl.CostEstimate(flops=400_000_000, bytes_accessed=6_000_000, transcendentals=0),
+        name="outputs",
+    )(x_all.reshape(256, half), act.reshape(256, 384), slots, sel)
+    return (layer_out, token_grad, gg[None], gu[None], gd[None])
+
+
 def solution(mesh):
+    sizes = (mesh.shape["dp"], mesh.shape["expert"])
     return jax.shard_map(
-        per_device,
+        per_device_fused if sizes == (2, 16) else per_device,
         mesh=mesh,
         in_specs=(
             P(("dp", "expert"), None),

time: 123 us -> 48.6 us (0.40)
  Pallas kernels: 0 us -> 40.6 us
  blocking collectives: 39.9 us -> 0 us
  waiting for transfers between devices: 23.2 us -> 0 us
  between operations: 14.2 us -> 0.66 us
  starting transfers between devices: 12.7 us -> 0 us
  matrix products: 12.4 us -> 0 us
  other arithmetic: 7.48 us -> 0 us
  local copies, waits for them, and re-layouts: 12.8 us -> 6.87 us
    pallas_call x0 -> x2, Pallas kernels: none -> 40.6 us  [the longest x1 38 us: per_device_fused(): pl.pallas_call(exchange_kernel, out_shape=(jax.ShapeDtypeStruct((16, 16,...]
    all_gather x3 -> x0, blocking collectives: 39.9 us -> none  [the longest x1 13.7 us: per_device(): lax.all_gather(w_down, 'dp', axis=1, tiled=True)]
    all_to_all x2 -> x0, waiting for transfers between devices: 20.5 us -> none  [the longest x1 20.5 us: per_device(): lax.all_to_all(results[0].astype(jnp.bfloat16), 'expert', split_axis=0, c...]
    all_to_all x2 -> x0, starting transfers between devices: 12.7 us -> none  [the longest x1 7.4 us: per_device(): lax.all_to_all(outgoing, 'expert', split_axis=0, concat_axis=0, tiled=True)]
    dot_general x13 -> x0, matrix products: 12.4 us -> none  [the longest x1 2.39 us: expert_math(): jnp.einsum('rh,pfh->prf', hidden, down_w, preferred_element_type=jnp.floa...]
    convert_element_type x4 -> x0, other arithmetic: 4.79 us -> none  [the longest x1 1.74 us: per_device(): term.astype(jnp.bfloat16)]
    another operation x4 -> x0, local copies, waits for them, and re-layouts: 3.23 us -> none
    reduce_scatter x1 -> x0, waiting for transfers between devices: 2.73 us -> none  [per_device(): lax.psum_scatter(term.astype(jnp.bfloat16), 'dp', scatter_dimension=0, ti...]
  transfers between devices with their start and end apart: 3 -> 0, of which waited for: 2 -> 0; matrix products, arithmetic and copies ran while one was open for 8% -> 0% of each run, Pallas kernels for 0% -> 0%
where the time goes in v1:
time: 48.6 us; the launch traced here: 48.2 us
  Pallas kernels  40.6 us (84%)
  local copies, waits for them, and re-layouts  6.87 us (14%)
  between operations  0.66 us (1%)
    pallas_call x1, Pallas kernels, per_device_fused(): pl.pallas_call(exchange_kernel, out_shape=(jax.ShapeDtypeStruct((16, 16,...  38 us
    unnamed x16, local copies, waits for them, and re-layouts  6.87 us
    pallas_call x1, Pallas kernels, per_device_fused(): pl.pallas_call(output_kernel, grid=(steps,), out_shape=(jax.ShapeDtypeStr...  2.63 us

profile of v1, /device:TPU:0, one launch (start us, length us, event | category | flops | bytes accessed | tf_op | source)
XLA Modules:
  0.0 48.2 jit_solution(9397227862219274993)
XLA Ops:
  0.6 0.0 copy-start.5
  0.6 0.7 %copy-done.5 = s32[128,8]{0,1:T(8,128)S(1)} copy-done((s32[128,8]{0,1:T(8,128)S(1)}, s32[128,8]{0,1:T(8,128)}, u32[]{:S(2)}) %copy-start.5) | copy-done | bytes 4120
  1.3 0.0 copy-start.6
  1.3 0.1 copy.12.ids_ref
  1.4 0.6 %copy-done.6 = s32[128,8]{0,1:T(8,128)S(1)} copy-done((s32[128,8]{0,1:T(8,128)S(1)}, s32[128,8]{0,1:T(8,128)}, u32[]{:S(2)}) %copy-start.6) | copy-done | bytes 4120
  2.0 0.1 copy.13.gates_ref
  2.1 0.0 copy-start
  2.1 1.2 %copy-done = bf16[128,3584]{1,0:T(8,128)(2,1)S(1)} copy-done((bf16[128,3584]{1,0:T(8,128)(2,1)S(1)}, bf16[128,3584]{1,0:T(8,128)(2,1)}, u32[]{:S(2)}) %copy-start) | copy-done | bytes 917528
  3.3 0.0 copy-start.1
  3.3 1.2 %copy-done.1 = bf16[128,3584]{1,0:T(8,128)(2,1)S(1)} copy-done((bf16[128,3584]{1,0:T(8,128)(2,1)S(1)}, bf16[128,3584]{1,0:T(8,128)(2,1)}, u32[]{:S(2)}) %copy-start.1) | copy-done | bytes 917528
  4.5 0.0 copy-start.2
  4.5 1.0 %copy-done.2 = bf16[1,1792,128]{2,1,0:T(8,128)(2,1)S(1)} copy-done((bf16[1,1792,128]{2,1,0:T(8,128)(2,1)S(1)}, bf16[1,1792,128]{2,1,0:T(8,128)(2,1)}, u32[]{:S(2)}) %copy-start.2) | copy-done | bytes 458776
  5.5 0.0 copy-start.3
  5.5 1.0 %copy-done.3 = bf16[1,1792,128]{2,1,0:T(8,128)(2,1)S(1)} copy-done((bf16[1,1792,128]{2,1,0:T(8,128)(2,1)S(1)}, bf16[1,1792,128]{2,1,0:T(8,128)(2,1)}, u32[]{:S(2)}) %copy-start.3) | copy-done | bytes 458776
  6.5 0.0 copy-start.4
  6.5 1.0 %copy-done.4 = bf16[1,1792,128]{2,1,0:T(8,128)(2,1)S(1)} copy-done((bf16[1,1792,128]{2,1,0:T(8,128)(2,1)S(1)}, bf16[1,1792,128]{2,1,0:T(8,128)(2,1)}, u32[]{:S(2)}) %copy-start.4) | copy-done | bytes 458776
  7.5 38.0 %exchange.1 = (bf16[16,16,1792]{2,1,0:T(8,128)(2,1)S(1)}, bf16[16,16,384]{2,1,0:T(8,128)(2,1)S(1)}, f32[8,3584]{1,0:T(8,128)S(1)}, bf16[128,128]{1,0:T(8,128)(2,1)S(1)}) custom-call(s32[128,8]{1,0:T(8,128)S(1)} %copy.12.ids_ref, s32[128,8]{1,0:T(8,128)S(1)} %copy.13.gates_ref, bf16[128,3584]{1,0:T(8,128)(2,1)S(1)} %copy-done, ...), custom_call_target="tpu_custom_call" | custom-call | flops 400000000 | bytes 6000000 | tf_op jit(solution)/shard_map/exchange/pallas_call | solution.py:348
  45.5 2.6 %outputs.1 = (bf16[128,3584]{1,0:T(8,128)(2,1)}, bf16[128,3584]{1,0:T(8,128)(2,1)}, f32[1792,128]{1,0:T(8,128)}, f32[1792,128]{1,0:T(8,128)}, f32[1792,128]{1,0:T(8,128)}) custom-call(bf16[256,1792]{1,0:T(8,128)(2,1)S(1)} %bitcast.11, bf16[256,384]{1,0:T(8,128)(2,1)S(1)} %bitcast.12, f32[8,3584]{1,0:T(8,128)S(1)} %get-tuple-element.16.slot_ref, ...), custom_call_target="tpu_custom_call" | custom-call | flops 400000000 | bytes 6000000 | tf_op jit(solution)/shard_map/outputs/pallas_call | solution.py:389
Async XLA Ops:
  0.6 0.7 %copy-start.5 = (s32[128,8]{0,1:T(8,128)S(1)}, s32[128,8]{0,1:T(8,128)}, u32[]{:S(2)}) copy-start(s32[128,8]{0,1:T(8,128)} %param.9) | copy-start | bytes 12292
  1.3 0.7 %copy-start.6 = (s32[128,8]{0,1:T(8,128)S(1)}, s32[128,8]{0,1:T(8,128)}, u32[]{:S(2)}) copy-start(s32[128,8]{0,1:T(8,128)} %param.10) | copy-start | bytes 12292
  2.1 1.2 %copy-start = (bf16[128,3584]{1,0:T(8,128)(2,1)S(1)}, bf16[128,3584]{1,0:T(8,128)(2,1)}, u32[]{:S(2)}) copy-start(bf16[128,3584]{1,0:T(8,128)(2,1)} %tok_hbm.1) | copy-start | bytes 2752516
  3.3 1.2 %copy-start.1 = (bf16[128,3584]{1,0:T(8,128)(2,1)S(1)}, bf16[128,3584]{1,0:T(8,128)(2,1)}, u32[]{:S(2)}) copy-start(bf16[128,3584]{1,0:T(8,128)(2,1)} %cot_hbm.1) | copy-start | bytes 2752516
  4.5 1.0 %copy-start.2 = (bf16[1,1792,128]{2,1,0:T(8,128)(2,1)S(1)}, bf16[1,1792,128]{2,1,0:T(8,128)(2,1)}, u32[]{:S(2)}) copy-start(bf16[1,1792,128]{2,1,0:T(8,128)(2,1)} %param.11) | copy-start | bytes 1376260
  5.5 1.0 %copy-start.3 = (bf16[1,1792,128]{2,1,0:T(8,128)(2,1)S(1)}, bf16[1,1792,128]{2,1,0:T(8,128)(2,1)}, u32[]{:S(2)}) copy-start(bf16[1,1792,128]{2,1,0:T(8,128)(2,1)} %param.12) | copy-start | bytes 1376260
  6.5 1.0 %copy-start.4 = (bf16[1,1792,128]{2,1,0:T(8,128)(2,1)S(1)}, bf16[1,1792,128]{2,1,0:T(8,128)(2,1)}, u32[]{:S(2)}) copy-start(bf16[1,1792,128]{2,1,0:T(8,128)(2,1)} %param.13) | copy-start | bytes 1376260

commit v2 on v1

--- a/solution.py
+++ b/solution.py
@@ -135,10 +135,10 @@
 
 
 def exchange_kernel(
-    ids_ref, gates_ref, tok_hbm, cot_hbm, wg_hbm, wu_hbm, wd_hbm,
+    ids_hbm, gates_hbm, tok_hbm, cot_hbm, wg_hbm, wu_hbm, wd_hbm,
     x_out, act_out, slot_out, sel_out,
-    tok_v, cot_v, w_v, gath, act_v, part, pex_s, pex_r, res, ra, sb, rb, sc, rc,
-    ys, yr, ys2, yr2, load_sem, send_sem, recv_sem,
+    ids_v, gates_v, both_v, w_v, gath, rows_v, act_v, part, pex_s, pex_r, res, ra, sb, rb, sc, rc,
+    across, load_sem, send_sem, recv_sem,
 ):
     y = lax.axis_index("dp")
     e = lax.axis_index("expert")
@@ -154,7 +154,7 @@
     peer_y = (1 - y, e)
     peer_c = (y, dev(z, x, 1 - c))
     peer_x = (y, dev(z, 1 - x, c))
-    peer_z = [None] + [(y, dev(zz, x, c)) for zz in near[1:]]
+    line = [[(yy, dev(zz, x, c)) for zz in near] for yy in (y, 1 - y)]
 
     started = []
 
@@ -168,71 +168,64 @@
         started.append(copy)
         return copy
 
+    n_tok = tok_hbm.shape[0]
     loads = [
-        pltpu.make_async_copy(tok_hbm, tok_v, load_sem.at[0]),
-        pltpu.make_async_copy(cot_hbm, cot_v, load_sem.at[1]),
-        pltpu.make_async_copy(wg_hbm, w_v.at[:, 0:128], load_sem.at[2]),
-        pltpu.make_async_copy(wu_hbm, w_v.at[:, 128:256], load_sem.at[3]),
-        pltpu.make_async_copy(wd_hbm, w_v.at[:, 256:384], load_sem.at[4]),
+        pltpu.make_async_copy(ids_hbm, ids_v, load_sem.at[0]),
+        pltpu.make_async_copy(gates_hbm, gates_v, load_sem.at[1]),
+        pltpu.make_async_copy(tok_hbm, both_v.at[:n_tok], load_sem.at[2]),
+        pltpu.make_async_copy(cot_hbm, both_v.at[n_tok:], load_sem.at[3]),
+        pltpu.make_async_copy(wg_hbm, w_v.at[:, 0:128], load_sem.at[4]),
+        pltpu.make_async_copy(wu_hbm, w_v.at[:, 128:256], load_sem.at[5]),
+        pltpu.make_async_copy(wd_hbm, w_v.at[:, 256:384], load_sem.at[6]),
     ]
     for load in loads:
         load.start()
     barrier = pltpu.get_barrier_semaphore()
-    greeted = [peer_y, peer_c, peer_x] + peer_z[1:]
+    greeted = [peer_c, peer_x] + line[0][1:] + line[1]
     for target in greeted:
         pl.semaphore_signal(barrier, inc=1, device_id=target, device_id_type=MESH)
 
-    hits = ids_ref[...] == 0
-    member = jnp.sum(jnp.where(hits, 1.0, 0.0), axis=1, keepdims=True)
-    weight = jnp.sum(jnp.where(hits, gates_ref[...].astype(F32), 0.0), axis=1, keepdims=True) * SCALE
-    n_tok = member.shape[0]
     square = (n_tok, n_tok)
-    lane = lax.broadcasted_iota(jnp.int32, square, 1)
-    earlier = jnp.where(lane < row_ids(square), 1.0, 0.0).astype(BF16)
-    spread = jnp.broadcast_to(member, square)
-    rank = jnp.dot(earlier, spread.astype(BF16), preferred_element_type=F32)
-    wanted = jnp.where(lane < 2 * CAP, lane % CAP, n_tok).astype(F32)
-    sel = jnp.where(jnp.logical_and(rank == wanted, spread > 0.5), 1.0, 0.0)
-    sel_out[...] = sel.astype(BF16)
-    sel_t = jnp.transpose(sel)[:8].astype(BF16)
-    gate8 = jnp.sum(jnp.transpose(sel * weight)[:8], axis=1, keepdims=True)
-
+    before = jnp.where(row_ids(square) < lax.broadcasted_iota(jnp.int32, square, 1), 1.0, 0.0).astype(BF16)
     loads[0].wait()
-    tok8 = jnp.dot(sel_t, tok_v[...], preferred_element_type=F32)
     loads[1].wait()
-    cot8 = jnp.dot(sel_t, cot_v[...], preferred_element_type=F32) * gate8
-    half = tok8.shape[1] // 2
+    hits = ids_v[...] == 0
+    member = jnp.sum(jnp.where(hits, 1.0, 0.0), axis=0, keepdims=True)
+    weight = jnp.sum(jnp.where(hits, gates_v[...].astype(F32), 0.0), axis=0, keepdims=True) * SCALE
+    member8 = jnp.broadcast_to(member, (8, n_tok))
+    rank = jnp.dot(member8.astype(BF16), before, preferred_element_type=F32)
+    wanted = (row_ids((8, n_tok)) % CAP).astype(F32)
+    sel = jnp.where(jnp.logical_and(rank == wanted, member8 > 0.5), 1.0, 0.0)
+    sel_out[...] = sel
+    gate8 = jnp.sum(sel * weight, axis=1, keepdims=True)
+    nothing = jnp.zeros_like(sel)
+    pick = jnp.concatenate(
+        [jnp.concatenate([sel, nothing], axis=1), jnp.concatenate([nothing, sel], axis=1)], axis=0
+    ).astype(BF16)
+    loads[2].wait()
+    loads[3].wait()
+    slots = jnp.dot(pick, both_v[...], preferred_element_type=F32)
+    half = slots.shape[1] // 2
     low = row_ids((8, half)) < 4
-
-    def mine(v, flip=False):
-        first, second = v[:, :half], v[:, half:]
-        return jnp.where((y == 0) != flip, first, second)
-
-    ys[...] = fold(jnp.where(low, mine(tok8, True), mine(cot8, True))).astype(BF16)
+    piece_lo = jnp.where(low, slots[:8, :half], slots[8:, :half] * gate8)
+    piece_hi = jnp.where(low, slots[:8, half:], slots[8:, half:] * gate8)
+    here = pos(z, x, c)
+    gath[here, y] = fold(jnp.where(y == 0, piece_lo, piece_hi)).astype(BF16)
+    across[...] = fold(jnp.where(y == 0, piece_hi, piece_lo)).astype(BF16)
     pl.semaphore_wait(barrier, len(greeted))
-    swap = remote(ys, yr, peer_y)
-    own_tok, own_cot = mine(tok8), mine(cot8)
-    swap.wait_recv()
-    got = unfold(yr[...].astype(F32))
-    got_r = pltpu.roll(got, 4, 0)
-    own_rows = jnp.logical_xor(low, y != 0)
-    chunk = jnp.concatenate(
-        [
-            jnp.where(own_rows, own_tok, jnp.where(low, got, got_r)),
-            jnp.where(own_rows, own_cot, jnp.where(low, got_r, got)),
-        ],
-        axis=0,
-    )
-    here = pos(z, x, c)
-    gath[here] = chunk.astype(BF16)
-
-    over_z, over_x, over_c = [None], [], []
+
+    own = gath.at[here, y]
+    over_z = [[None] * 4, [None] * 4]
+    over_z[1][0] = remote(across, own, line[1][0])
     for k in (1, 2, 3):
-        over_z.append(remote(gath.at[here], gath.at[here], peer_z[k]))
+        over_z[0][k] = remote(own, own, line[0][k])
+        over_z[1][k] = remote(across, own, line[1][k])
+    over_x, over_c = [], []
     for k in range(4):
         at = pos(near[k], x, c)
-        if k:
-            over_z[k].wait_recv()
+        for copy in (over_z[0][k], over_z[1][k]):
+            if copy is not None:
+                copy.wait_recv()
         over_x.append(remote(gath.at[at], gath.at[at], peer_x))
         over_c.append(remote(gath.at[at], gath.at[at], peer_c))
     for k in range(4):
@@ -240,13 +233,23 @@
         over_x[k].wait_recv()
         over_c.append(remote(gath.at[at], gath.at[at], peer_c))
 
-    for load in loads[2:]:
+    for load in loads[4:]:
         load.wait()
 
+    low3 = lax.broadcasted_iota(jnp.int32, (8, 8, 384), 1) < 4
+
     def project(h):
-        rows = gath[pl.ds(h * 8, 8)].reshape(128, half)
-        p = jnp.dot(rows, w_v[...], preferred_element_type=F32).reshape(8, 16, 384)
-        both = jnp.concatenate([p[:, :8, :256], p[:, 8:, 256:]], axis=2).reshape(64, 384)
+        for n in range(8):
+            got = gath[h * 8 + n].astype(F32)
+            rows_v[h * 8 + n] = jnp.concatenate([unfold(got[0]), unfold(got[1])], axis=0).astype(BF16)
+        rows = rows_v[pl.ds(h * 8, 8)].reshape(128, half)
+        p = jnp.dot(rows, w_v[...], preferred_element_type=F32).reshape(8, 2, 8, 384)
+        p0, p1 = p[:, 0], p[:, 1]
+        down1 = pltpu.roll(p1.reshape(64, 384), 4, 0).reshape(8, 8, 384)
+        up0 = pltpu.roll(p0.reshape(64, 384), 60, 0).reshape(8, 8, 384)
+        tok_part = jnp.where(low3, p0, down1)
+        cot_part = jnp.where(low3, up0, p1)
+        both = jnp.concatenate([tok_part[:, :, :256], cot_part[:, :, 256:]], axis=2).reshape(64, 384)
         part[h] = both
         pex_s[h] = both.astype(BF16)
         return remote(pex_s.at[h], pex_r.at[h], peer_y)
@@ -266,15 +269,24 @@
         res[pl.ds(h * 8, 8)] = jnp.concatenate(
             [out.reshape(8, 8, half), grad.reshape(8, 8, half)], axis=1
         ).astype(BF16)
-        top = jnp.concatenate([d_both.astype(F32).reshape(8, 8, 256), jnp.zeros((8, 8, 128), F32)], axis=2)
-        bottom = jnp.concatenate([jnp.zeros((8, 8, 256), F32), hidden.astype(F32).reshape(8, 8, 128)], axis=2)
-        act_v[pl.ds(h * 8, 8)] = jnp.concatenate([top, bottom], axis=1).astype(BF16)
+        acts = jnp.concatenate([d_both, hidden], axis=1).astype(F32)
+        up = pltpu.roll(acts, 60, 0).reshape(8, 8, 384)
+        down = pltpu.roll(acts, 4, 0).reshape(8, 8, 384)
+        acts = acts.reshape(8, 8, 384)
+        for_tok = lax.broadcasted_iota(jnp.int32, (8, 8, 384), 2) < 256
+        act_v[pl.ds(h * 8, 8)] = jnp.concatenate(
+            [
+                jnp.where(for_tok, jnp.where(low3, acts, 0.0), jnp.where(low3, 0.0, down)),
+                jnp.where(for_tok, jnp.where(low3, up, 0.0), jnp.where(low3, 0.0, acts)),
+            ],
+            axis=1,
+        ).astype(BF16)
 
     swap_own = project(c)
     for copy in over_c:
         copy.wait_recv()
     swap_other = project(1 - c)
-    keep_x = pltpu.make_async_copy(gath, x_out, load_sem.at[5])
+    keep_x = pltpu.make_async_copy(rows_v, x_out, load_sem.at[7])
     keep_x.start()
     swap_other.wait_recv()
     activate(1 - c)
@@ -284,7 +296,7 @@
         to_core.append(remote(src, ra.at[pl.ds(xx * 4, 4)], peer_c))
     swap_own.wait_recv()
     activate(c)
-    keep_act = pltpu.make_async_copy(act_v, act_out, load_sem.at[6])
+    keep_act = pltpu.make_async_copy(act_v, act_out, load_sem.at[8])
     keep_act.start()
     to_core[0].wait_recv()
     to_x = [None] * 4
@@ -298,27 +310,28 @@
         zz = near[k]
         mid = res[pos(zz, x, c)].astype(F32) + ra[x * 4 + zz].astype(F32)
         to_x[k].wait_recv()
-        return mid + rb[k].astype(F32)
-
-    to_z = [None] * 4
-    for k in (3, 2, 1):
-        sc[k] = summed(k).astype(BF16)
-        to_z[k] = remote(sc.at[k], rc.at[k], peer_z[k])
-    total = summed(0)
-    for k in (1, 2, 3):
-        to_z[k].wait_recv()
-        total = total + rc[k].astype(F32)
-    out8, grad8 = total[:8], total[8:]
-    for_0 = jnp.where(low, out8, pltpu.roll(grad8, 4, 0))
-    for_1 = jnp.where(low, pltpu.roll(out8, 4, 0), grad8)
-    ys2[...] = fold(jnp.where(y == 0, for_1, for_0)).astype(BF16)
-    swap = remote(ys2, yr2, peer_y)
-    mine8 = jnp.where(y == 0, for_0, for_1).astype(BF16).astype(F32)
+        mid = mid + rb[k].astype(F32)
+        out8, grad8 = mid[:8], mid[8:]
+        for_0 = jnp.where(low, out8, pltpu.roll(grad8, 4, 0))
+        for_1 = jnp.where(low, pltpu.roll(out8, 4, 0), grad8)
+        return jnp.where(y == 0, for_0, for_1), jnp.where(y == 0, for_1, for_0)
+
+    to_z = []
+    for k in (3, 2, 1, 0):
+        same, other = summed(k)
+        sc[1, k] = fold(other).astype(BF16)
+        to_z.append((1, k, remote(sc.at[1, k], rc.at[1, k], line[1][k])))
+        if k:
+            sc[0, k] = fold(same).astype(BF16)
+            to_z.append((0, k, remote(sc.at[0, k], rc.at[0, k], line[0][k])))
+    total = [same, jnp.zeros_like(same)]
+    for s_y, k, copy in to_z:
+        copy.wait_recv()
+        total[s_y] = total[s_y] + unfold(rc[s_y, k].astype(F32))
+    mine8, got8 = (t.astype(BF16).astype(F32) for t in total)
     scale = jnp.where(row_ids((8, 1)) < 4, gate8, 1.0)
-    swap.wait_recv()
-    got = unfold(yr2[...].astype(F32))
-    slot_out[:, :half] = jnp.where(y == 0, mine8, got) * scale
-    slot_out[:, half:] = jnp.where(y == 0, got, mine8) * scale
+    slot_out[:, :half] = jnp.where(y == 0, mine8, got8) * scale
+    slot_out[:, half:] = jnp.where(y == 0, got8, mine8) * scale
     keep_x.wait()
     keep_act.wait()
     for copy in started:
@@ -326,13 +339,13 @@
 
 
 def output_kernel(x_ref, act_ref, slot_ref, sel_ref, out_ref, tg_ref, gg_ref, gu_ref, gd_ref):
-    sel = sel_ref[...][:, :8].astype(F32)
-    lane = lax.broadcasted_iota(jnp.int32, sel.shape, 1)
+    sel = sel_ref[...]
+    low = row_ids(sel.shape) < 4
     slots = slot_ref[...].astype(BF16)
-    for ref, keep in ((out_ref, lane < 4), (tg_ref, lane >= 4)):
+    tn = (((0,), (0,)), ((), ()))
+    for ref, keep in ((out_ref, low), (tg_ref, jnp.logical_not(low))):
         picks = jnp.where(keep, sel, 0.0).astype(BF16)
-        ref[...] = jnp.dot(picks, slots, preferred_element_type=F32).astype(BF16)
-    tn = (((0,), (0,)), ((), ()))
+        ref[...] = lax.dot_general(picks, slots, tn, preferred_element_type=F32).astype(BF16)
     grads = lax.dot_general(x_ref[...], act_ref[...], tn, preferred_element_type=F32)
     for n, ref in enumerate((gg_ref, gu_ref, gd_ref)):
         ref[...] = grads[:, n * 128 : (n + 1) * 128]
@@ -341,24 +354,27 @@
 def per_device_fused(tokens, out_cotangent, expert_ids, gate_fixed, w_gate, w_up, w_down):
     n_tok, width = tokens.shape
     half = width // 2
-    hbm = pl.BlockSpec(memory_space=pl.ANY)
+    hbm = pl.BlockSpec(memory_space=pltpu.HBM)
     vmem = pl.BlockSpec(memory_space=pltpu.VMEM)
-    copies = 28
+    copies = 35
     chunks = lambda n: pltpu.VMEM((n, 16, half), BF16)
+    pieces = lambda m, n: pltpu.VMEM((m, n, 16, half // 2), BF16)
     x_all, act, slots, sel = pl.pallas_call(
         exchange_kernel,
         out_shape=(
             jax.ShapeDtypeStruct((16, 16, half), BF16),
             jax.ShapeDtypeStruct((16, 16, 384), BF16),
             jax.ShapeDtypeStruct((8, width), F32),
-            jax.ShapeDtypeStruct((n_tok, n_tok), BF16),
+            jax.ShapeDtypeStruct((8, n_tok), F32),
         ),
-        in_specs=[vmem] * 2 + [hbm] * 5,
+        in_specs=[hbm] * 7,
         out_specs=(hbm, hbm, vmem, vmem),
         scratch_shapes=[
-            pltpu.VMEM((n_tok, width), BF16),
-            pltpu.VMEM((n_tok, width), BF16),
+            pltpu.VMEM(expert_ids.shape[::-1], jnp.int32),
+            pltpu.VMEM(gate_fixed.shape[::-1], jnp.int32),
+            pltpu.VMEM((2 * n_tok, width), BF16),
             pltpu.VMEM((half, 384), BF16),
+            pieces(16, 2),
             chunks(16),
             pltpu.VMEM((16, 16, 384), BF16),
             pltpu.VMEM((2, 64, 384), F32),
@@ -368,21 +384,19 @@
             chunks(8),
             chunks(4),
             chunks(4),
-            chunks(4),
-            chunks(4),
-        ]
-        + [pltpu.VMEM((16, half // 2), BF16)] * 4
-        + [
-            pltpu.SemaphoreType.DMA((7,)),
+            pieces(2, 4),
+            pieces(2, 4),
+            pltpu.VMEM((16, half // 2), BF16),
+            pltpu.SemaphoreType.DMA((9,)),
             pltpu.SemaphoreType.DMA((copies,)),
             pltpu.SemaphoreType.DMA((copies,)),
         ],
         compiler_params=pltpu.CompilerParams(
-            collective_id=0, has_side_effects=True, vmem_limit_bytes=40 * 1024 * 1024
+            collective_id=0, has_side_effects=True, vmem_limit_bytes=60 * 1024 * 1024
         ),
         cost_estimate=pl.CostEstimate(flops=400_000_000, bytes_accessed=6_000_000, transcendentals=16384),
         name="exchange",
-    )(expert_ids, gate_fixed, tokens, out_cotangent, w_gate[0], w_up[0], w_down[0])
+    )(expert_ids.T, gate_fixed.T, tokens, out_cotangent, w_gate[0], w_up[0], w_down[0])
     steps = 2
     grad_spec = pl.BlockSpec((half // steps, 128), lambda i: (i, 0))
     tok_spec = pl.BlockSpec((n_tok, width // steps), lambda i: (0, i))
@@ -395,10 +409,10 @@
             pl.BlockSpec((256, half // steps), lambda i: (0, i)),
             pl.BlockSpec((256, 384), lambda i: (0, 0)),
             pl.BlockSpec((8, width // steps), lambda i: (0, i)),
-            pl.BlockSpec((n_tok, n_tok), lambda i: (0, 0)),
+            pl.BlockSpec((8, n_tok), lambda i: (0, 0)),
         ],
         out_specs=(tok_spec, tok_spec, grad_spec, grad_spec, grad_spec),
-        compiler_params=pltpu.CompilerParams(vmem_limit_bytes=32 * 1024 * 1024),
+        compiler_params=pltpu.CompilerParams(vmem_limit_bytes=60 * 1024 * 1024),
         cost_estimate=pl.CostEstimate(flops=400_000_000, bytes_accessed=6_000_000, transcendentals=0),
         name="outputs",
     )(x_all.reshape(256, half), act.reshape(256, 384), slots, sel)

time: 48.6 us -> 38.3 us (0.79)
  local copies, waits for them, and re-layouts: 6.87 us -> 0 us
  Pallas kernels: 40.6 us -> 37.5 us
    unnamed x16 -> x0, local copies, waits for them, and re-layouts: 6.87 us -> none
    pallas_call x1, Pallas kernels: 38 us -> 33.9 us  [per_device_fused(): pl.pallas_call(exchange_kernel, out_shape=(jax.ShapeDtypeStruct((16, 16,...]
    pallas_call x1, Pallas kernels: 2.63 us -> 3.61 us  [per_device_fused(): pl.pallas_call(output_kernel, grid=(steps,), out_shape=(jax.ShapeDtypeStr...]
where the time goes in v2:
time: 38.3 us; the launch traced here: 38.1 us
  Pallas kernels  37.5 us (98%)
  between operations  0.64 us (2%)
    pallas_call x1, Pallas kernels, per_device_fused(): pl.pallas_call(exchange_kernel, out_shape=(jax.ShapeDtypeStruct((16, 16,...  33.9 us
    pallas_call x1, Pallas kernels, per_device_fused(): pl.pallas_call(output_kernel, grid=(steps,), out_shape=(jax.ShapeDtypeStr...  3.61 us

profile of v2, /device:TPU:0, one launch (start us, length us, event | category | flops | bytes accessed | tf_op | source)
XLA Modules:
  0.0 38.1 jit_solution(5720630511826610794)
XLA Ops:
  0.6 33.9 %exchange.1 = (bf16[16,16,1792]{2,1,0:T(8,128)(2,1)}, bf16[16,16,384]{2,1,0:T(8,128)(2,1)}, f32[8,3584]{1,0:T(8,128)}, f32[8,128]{1,0:T(8,128)}) custom-call(s32[8,128]{1,0:T(8,128)} %bitcast.13, s32[8,128]{1,0:T(8,128)} %bitcast.14, bf16[128,3584]{1,0:T(8,128)(2,1)} %tok_hbm.1, bf16[128,3584]{1,0:T(8,128)(2,1)} %cot_hbm.1, bf16[1792,128]{1,0:T(8,128)(2,1)} %bitcast.10, ...), custom_call_target="tpu_custom_call" | custom-call | flops 400000000 | bytes 6000000 | tf_op jit(solution)/shard_map/exchange/pallas_call | solution.py:362
  34.5 3.6 %outputs.1 = (bf16[128,3584]{1,0:T(8,128)(2,1)}, bf16[128,3584]{1,0:T(8,128)(2,1)}, f32[1792,128]{1,0:T(8,128)}, f32[1792,128]{1,0:T(8,128)}, f32[1792,128]{1,0:T(8,128)}) custom-call(bf16[256,1792]{1,0:T(8,128)(2,1)} %bitcast.15, bf16[256,384]{1,0:T(8,128)(2,1)} %bitcast.16, f32[8,3584]{1,0:T(8,128)} %get-tuple-element.16.slot_ref, ...), custom_call_target="tpu_custom_call" | custom-call | flops 400000000 | bytes 6000000 | tf_op jit(solution)/shard_map/outputs/pallas_call | solution.py:403

commit v3 on v2

--- a/solution.py
+++ b/solution.py
@@ -136,9 +136,9 @@
 
 def exchange_kernel(
     ids_hbm, gates_hbm, tok_hbm, cot_hbm, wg_hbm, wu_hbm, wd_hbm,
-    x_out, act_out, slot_out, sel_out,
+    gg_out, gu_out, gd_out, slot_out, sel_out,
     ids_v, gates_v, both_v, w_v, gath, rows_v, act_v, part, pex_s, pex_r, res, ra, sb, rb, sc, rc,
-    across, load_sem, send_sem, recv_sem,
+    across, grad_v, load_sem, send_sem, recv_sem,
 ):
     y = lax.axis_index("dp")
     e = lax.axis_index("expert")
@@ -148,7 +148,7 @@
         return zz * 4 + xx * 2 + cc
 
     def pos(zz, xx, cc):
-        return cc * 8 + xx * 4 + zz
+        return (zz // 2) * 8 + cc * 4 + xx * 2 + zz % 2
 
     near = [z, z + 1 - 2 * (z % 2), (z + 2) % 4, 3 - z]
     peer_y = (1 - y, e)
@@ -216,25 +216,24 @@
 
     own = gath.at[here, y]
     over_z = [[None] * 4, [None] * 4]
-    over_z[1][0] = remote(across, own, line[1][0])
-    for k in (1, 2, 3):
-        over_z[0][k] = remote(own, own, line[0][k])
+    for k in (1, 0, 2, 3):
+        if k:
+            over_z[0][k] = remote(own, own, line[0][k])
         over_z[1][k] = remote(across, own, line[1][k])
-    over_x, over_c = [], []
-    for k in range(4):
+    over_x, over_c = [], [[], []]
+
+    def forward(k):
         at = pos(near[k], x, c)
         for copy in (over_z[0][k], over_z[1][k]):
             if copy is not None:
                 copy.wait_recv()
         over_x.append(remote(gath.at[at], gath.at[at], peer_x))
-        over_c.append(remote(gath.at[at], gath.at[at], peer_c))
-    for k in range(4):
+        over_c[k // 2].append(remote(gath.at[at], gath.at[at], peer_c))
+
+    def forward_x(k):
         at = pos(near[k], 1 - x, c)
         over_x[k].wait_recv()
-        over_c.append(remote(gath.at[at], gath.at[at], peer_c))
-
-    for load in loads[4:]:
-        load.wait()
+        over_c[k // 2].append(remote(gath.at[at], gath.at[at], peer_c))
 
     low3 = lax.broadcasted_iota(jnp.int32, (8, 8, 384), 1) < 4
 
@@ -282,33 +281,40 @@
             axis=1,
         ).astype(BF16)
 
-    swap_own = project(c)
-    for copy in over_c:
-        copy.wait_recv()
-    swap_other = project(1 - c)
-    keep_x = pltpu.make_async_copy(rows_v, x_out, load_sem.at[7])
-    keep_x.start()
-    swap_other.wait_recv()
-    activate(1 - c)
-    to_core = []
-    for xx in (1 - x, x):
-        src = res.at[pl.ds((1 - c) * 8 + xx * 4, 4)]
-        to_core.append(remote(src, ra.at[pl.ds(xx * 4, 4)], peer_c))
-    swap_own.wait_recv()
-    activate(c)
-    keep_act = pltpu.make_async_copy(act_v, act_out, load_sem.at[8])
-    keep_act.start()
-    to_core[0].wait_recv()
+    def core_chunks(part_of):
+        for copy in over_c[part_of]:
+            copy.wait_recv()
+
+    def to_core(pair):
+        src = res.at[pl.ds(pair * 8 + (1 - c) * 4, 4)]
+        return remote(src, ra.at[pl.ds(pair * 4, 4)], peer_c)
+
+    def core_sum(k, xx):
+        zz = near[k]
+        return res[pos(zz, xx, c)].astype(F32) + ra[(zz // 2) * 4 + xx * 2 + zz % 2].astype(F32)
+
     to_x = [None] * 4
-    for k in (3, 2, 1, 0):
-        zz = near[k]
-        sb[k] = (res[pos(zz, 1 - x, c)].astype(F32) + ra[(1 - x) * 4 + zz].astype(F32)).astype(BF16)
+
+    def send_x(k):
+        sb[k] = core_sum(k, 1 - x).astype(BF16)
         to_x[k] = remote(sb.at[k], rb.at[k], peer_x)
-    to_core[1].wait_recv()
+
+    grad_copies = []
+
+    def gradients(n):
+        cols = half // 2
+        rows = rows_v[:, :, n * cols : (n + 1) * cols].reshape(256, cols)
+        tn = (((0,), (0,)), ((), ()))
+        terms = lax.dot_general(rows, act_v[...].reshape(256, 384), tn, preferred_element_type=F32)
+        for i, out in enumerate((gg_out, gu_out, gd_out)):
+            at = pl.ds(n * cols, cols)
+            grad_v[i, at] = terms[:, i * 128 : (i + 1) * 128]
+            copy = pltpu.make_async_copy(grad_v.at[i, at], out.at[at], load_sem.at[7 + 3 * n + i])
+            copy.start()
+            grad_copies.append(copy)
 
     def summed(k):
-        zz = near[k]
-        mid = res[pos(zz, x, c)].astype(F32) + ra[x * 4 + zz].astype(F32)
+        mid = core_sum(k, x)
         to_x[k].wait_recv()
         mid = mid + rb[k].astype(F32)
         out8, grad8 = mid[:8], mid[8:]
@@ -317,13 +323,49 @@
         return jnp.where(y == 0, for_0, for_1), jnp.where(y == 0, for_1, for_0)
 
     to_z = []
-    for k in (3, 2, 1, 0):
+
+    def send_z(k):
         same, other = summed(k)
         sc[1, k] = fold(other).astype(BF16)
         to_z.append((1, k, remote(sc.at[1, k], rc.at[1, k], line[1][k])))
         if k:
             sc[0, k] = fold(same).astype(BF16)
             to_z.append((0, k, remote(sc.at[0, k], rc.at[0, k], line[0][k])))
+        return same
+
+    pair = z // 2
+    forward(0)
+    forward(1)
+    forward_x(0)
+    forward_x(1)
+    forward(2)
+    for load in loads[4:]:
+        load.wait()
+    core_chunks(0)
+    swap_near = project(pair)
+    forward(3)
+    forward_x(2)
+    forward_x(3)
+    core_chunks(1)
+    swap_far = project(1 - pair)
+    swap_near.wait_recv()
+    activate(pair)
+    core_near = to_core(pair)
+    core_near.wait_recv()
+    send_x(1)
+    send_x(0)
+    swap_far.wait_recv()
+    activate(1 - pair)
+    core_far = to_core(1 - pair)
+    gradients(0)
+    core_far.wait_recv()
+    send_x(3)
+    send_x(2)
+    send_z(1)
+    same = send_z(0)
+    gradients(1)
+    send_z(3)
+    send_z(2)
     total = [same, jnp.zeros_like(same)]
     for s_y, k, copy in to_z:
         copy.wait_recv()
@@ -332,23 +374,34 @@
     scale = jnp.where(row_ids((8, 1)) < 4, gate8, 1.0)
     slot_out[:, :half] = jnp.where(y == 0, mine8, got8) * scale
     slot_out[:, half:] = jnp.where(y == 0, got8, mine8) * scale
-    keep_x.wait()
-    keep_act.wait()
+    for copy in grad_copies:
+        copy.wait()
     for copy in started:
         copy.wait_send()
 
 
-def output_kernel(x_ref, act_ref, slot_ref, sel_ref, out_ref, tg_ref, gg_ref, gu_ref, gd_ref):
+def output_kernel(slot_ref, sel_ref, gg_in, gu_in, gd_in, out_ref, tg_ref, gg_ref, gu_ref, gd_ref, rows, sems):
+    copies = []
+
+    def move(src, dst):
+        copy = pltpu.make_async_copy(src, dst, sems.at[len(copies)])
+        copy.start()
+        copies.append(copy)
+
+    cut = gg_in.shape[0] // 2
+    for n in range(2):
+        for src, dst in ((gg_in, gg_ref), (gu_in, gu_ref), (gd_in, gd_ref)):
+            move(src.at[pl.ds(n * cut, cut)], dst.at[pl.ds(n * cut, cut)])
     sel = sel_ref[...]
     low = row_ids(sel.shape) < 4
     slots = slot_ref[...].astype(BF16)
     tn = (((0,), (0,)), ((), ()))
-    for ref, keep in ((out_ref, low), (tg_ref, jnp.logical_not(low))):
+    for n, (ref, keep) in enumerate(((out_ref, low), (tg_ref, jnp.logical_not(low)))):
         picks = jnp.where(keep, sel, 0.0).astype(BF16)
-        ref[...] = lax.dot_general(picks, slots, tn, preferred_element_type=F32).astype(BF16)
-    grads = lax.dot_general(x_ref[...], act_ref[...], tn, preferred_element_type=F32)
-    for n, ref in enumerate((gg_ref, gu_ref, gd_ref)):
-        ref[...] = grads[:, n * 128 : (n + 1) * 128]
+        rows[n] = lax.dot_general(picks, slots, tn, preferred_element_type=F32).astype(BF16)
+        move(rows.at[n], ref)
+    for copy in copies:
+        copy.wait()
 
 
 def per_device_fused(tokens, out_cotangent, expert_ids, gate_fixed, w_gate, w_up, w_down):
@@ -359,16 +412,15 @@
     copies = 35
     chunks = lambda n: pltpu.VMEM((n, 16, half), BF16)
     pieces = lambda m, n: pltpu.VMEM((m, n, 16, half // 2), BF16)
-    x_all, act, slots, sel = pl.pallas_call(
+    gg, gu, gd, slots, sel = pl.pallas_call(
         exchange_kernel,
         out_shape=(
-            jax.ShapeDtypeStruct((16, 16, half), BF16),
-            jax.ShapeDtypeStruct((16, 16, 384), BF16),
+            *[jax.ShapeDtypeStruct((half, 128), F32)] * 3,
             jax.ShapeDtypeStruct((8, width), F32),
             jax.ShapeDtypeStruct((8, n_tok), F32),
         ),
         in_specs=[hbm] * 7,
-        out_specs=(hbm, hbm, vmem, vmem),
+        out_specs=(hbm, hbm, hbm, vmem, vmem),
         scratch_shapes=[
             pltpu.VMEM(expert_ids.shape[::-1], jnp.int32),
             pltpu.VMEM(gate_fixed.shape[::-1], jnp.int32),
@@ -387,7 +439,8 @@
             pieces(2, 4),
             pieces(2, 4),
             pltpu.VMEM((16, half // 2), BF16),
-            pltpu.SemaphoreType.DMA((9,)),
+            pltpu.VMEM((3, half, 128), F32),
+            pltpu.SemaphoreType.DMA((13,)),
             pltpu.SemaphoreType.DMA((copies,)),
             pltpu.SemaphoreType.DMA((copies,)),
         ],
@@ -397,25 +450,17 @@
         cost_estimate=pl.CostEstimate(flops=400_000_000, bytes_accessed=6_000_000, transcendentals=16384),
         name="exchange",
     )(expert_ids.T, gate_fixed.T, tokens, out_cotangent, w_gate[0], w_up[0], w_down[0])
-    steps = 2
-    grad_spec = pl.BlockSpec((half // steps, 128), lambda i: (i, 0))
-    tok_spec = pl.BlockSpec((n_tok, width // steps), lambda i: (0, i))
     layer_out, token_grad, gg, gu, gd = pl.pallas_call(
         output_kernel,
-        grid=(steps,),
         out_shape=(jax.ShapeDtypeStruct((n_tok, width), BF16),) * 2
         + (jax.ShapeDtypeStruct((half, 128), F32),) * 3,
-        in_specs=[
-            pl.BlockSpec((256, half // steps), lambda i: (0, i)),
-            pl.BlockSpec((256, 384), lambda i: (0, 0)),
-            pl.BlockSpec((8, width // steps), lambda i: (0, i)),
-            pl.BlockSpec((8, n_tok), lambda i: (0, 0)),
-        ],
-        out_specs=(tok_spec, tok_spec, grad_spec, grad_spec, grad_spec),
+        in_specs=[vmem, vmem, hbm, hbm, hbm],
+        out_specs=(hbm,) * 5,
+        scratch_shapes=[pltpu.VMEM((2, n_tok, width), BF16), pltpu.SemaphoreType.DMA((8,))],
         compiler_params=pltpu.CompilerParams(vmem_limit_bytes=60 * 1024 * 1024),
-        cost_estimate=pl.CostEstimate(flops=400_000_000, bytes_accessed=6_000_000, transcendentals=0),
+        cost_estimate=pl.CostEstimate(flops=15_000_000, bytes_accessed=8_000_000, transcendentals=0),
         name="outputs",
-    )(x_all.reshape(256, half), act.reshape(256, 384), slots, sel)
+    )(slots, sel, gg, gu, gd)
     return (layer_out, token_grad, gg[None], gu[None], gd[None])
 
 

time: 38.3 us -> 123 us (3.21)
  Pallas kernels: 37.5 us -> 122 us
    pallas_call x2, Pallas kernels: 37.5 us -> 122 us  [the longest x1 85.5 us: per_device_fused(): pl.pallas_call(output_kernel, out_shape=(jax.ShapeDtypeStruct((n_tok, wid...]
where the time goes in v3:
time: 123 us; the launch traced here: 122 us
  Pallas kernels  122 us (99%)
    pallas_call x1, Pallas kernels, per_device_fused(): pl.pallas_call(output_kernel, out_shape=(jax.ShapeDtypeStruct((n_tok, wid...  85.5 us
    pallas_call x1, Pallas kernels, per_device_fused(): pl.pallas_call(exchange_kernel, out_shape=(*[jax.ShapeDtypeStruct((half,...  36.3 us

profile of v3, /device:TPU:0, one launch (start us, length us, event | category | flops | bytes accessed | tf_op | source)
XLA Modules:
  0.0 122.4 jit_solution(6262553393388693179)
XLA Ops:
  0.6 36.3 %exchange.1 = (f32[1792,128]{1,0:T(8,128)}, f32[1792,128]{1,0:T(8,128)}, f32[1792,128]{1,0:T(8,128)}, f32[8,3584]{1,0:T(8,128)}, f32[8,128]{1,0:T(8,128)}) custom-call(s32[8,128]{1,0:T(8,128)} %bitcast.11, s32[8,128]{1,0:T(8,128)} %bitcast.12, bf16[128,3584]{1,0:T(8,128)(2,1)} %tok_hbm.1, bf16[128,3584]{1,0:T(8,128)(2,1)} %cot_hbm.1, ...), custom_call_target="tpu_custom_call" | custom-call | flops 400000000 | bytes 6000000 | tf_op jit(solution)/shard_map/exchange/pallas_call | solution.py:415
  36.9 85.5 %outputs.1 = (bf16[128,3584]{1,0:T(8,128)(2,1)}, bf16[128,3584]{1,0:T(8,128)(2,1)}, f32[1792,128]{1,0:T(8,128)}, f32[1792,128]{1,0:T(8,128)}, f32[1792,128]{1,0:T(8,128)}) custom-call(f32[8,3584]{1,0:T(8,128)} %get-tuple-element.15.slot_ref, f32[8,128]{1,0:T(8,128)} %get-tuple-element.16.sel_ref, f32[1792,128]{1,0:T(8,128)} %get-tuple-element.17.gg_in, ...), custom_call_target="tpu_custom_call" | custom-call | flops 15000000 | bytes 8000000 | tf_op jit(solution)/shard_map/outputs/pallas_call | solution.py:453

commit v4 on v3

--- a/solution.py
+++ b/solution.py
@@ -137,8 +137,8 @@
 def exchange_kernel(
     ids_hbm, gates_hbm, tok_hbm, cot_hbm, wg_hbm, wu_hbm, wd_hbm,
     gg_out, gu_out, gd_out, slot_out, sel_out,
-    ids_v, gates_v, both_v, w_v, gath, rows_v, act_v, part, pex_s, pex_r, res, ra, sb, rb, sc, rc,
-    across, grad_v, load_sem, send_sem, recv_sem,
+    ids_v, gates_v, both_v, w_v, w_t, gath, rows_v, act_v, part, pex_s, pex_r, res, ra, sb, rb, sc, rc,
+    across, mate_s, mate_r, grad_v, load_sem, send_sem, recv_sem,
 ):
     y = lax.axis_index("dp")
     e = lax.axis_index("expert")
@@ -216,7 +216,7 @@
 
     own = gath.at[here, y]
     over_z = [[None] * 4, [None] * 4]
-    for k in (1, 0, 2, 3):
+    for k in (2, 1, 0):
         if k:
             over_z[0][k] = remote(own, own, line[0][k])
         over_z[1][k] = remote(across, own, line[1][k])
@@ -227,6 +227,8 @@
         for copy in (over_z[0][k], over_z[1][k]):
             if copy is not None:
                 copy.wait_recv()
+        if k == 2:
+            over_z[0][3] = remote(gath.at[at], gath.at[at], line[0][1])
         over_x.append(remote(gath.at[at], gath.at[at], peer_x))
         over_c[k // 2].append(remote(gath.at[at], gath.at[at], peer_c))
 
@@ -262,9 +264,8 @@
         d_gate = (d_hidden * up_pre * sig * (1.0 + gate_pre * (1.0 - sig))).astype(BF16)
         d_up = (d_hidden * act).astype(BF16)
         d_both = jnp.concatenate([d_gate, d_up], axis=1)
-        nt = (((1,), (1,)), ((), ()))
-        out = lax.dot_general(hidden, w_v[:, 256:], nt, preferred_element_type=F32)
-        grad = lax.dot_general(d_both, w_v[:, :256], nt, preferred_element_type=F32)
+        out = jnp.dot(hidden, w_t[256:], preferred_element_type=F32)
+        grad = jnp.dot(d_both, w_t[:256], preferred_element_type=F32)
         res[pl.ds(h * 8, 8)] = jnp.concatenate(
             [out.reshape(8, 8, half), grad.reshape(8, 8, half)], axis=1
         ).astype(BF16)
@@ -302,7 +303,7 @@
     grad_copies = []
 
     def gradients(n):
-        cols = half // 2
+        cols = half // 7
         rows = rows_v[:, :, n * cols : (n + 1) * cols].reshape(256, cols)
         tn = (((0,), (0,)), ((), ()))
         terms = lax.dot_general(rows, act_v[...].reshape(256, 384), tn, preferred_element_type=F32)
@@ -316,7 +317,9 @@
     def summed(k):
         mid = core_sum(k, x)
         to_x[k].wait_recv()
-        mid = mid + rb[k].astype(F32)
+        return mid + rb[k].astype(F32)
+
+    def for_y(mid):
         out8, grad8 = mid[:8], mid[8:]
         for_0 = jnp.where(low, out8, pltpu.roll(grad8, 4, 0))
         for_1 = jnp.where(low, pltpu.roll(out8, 4, 0), grad8)
@@ -324,8 +327,8 @@
 
     to_z = []
 
-    def send_z(k):
-        same, other = summed(k)
+    def send_z(k, mid):
+        same, other = for_y(mid)
         sc[1, k] = fold(other).astype(BF16)
         to_z.append((1, k, remote(sc.at[1, k], rc.at[1, k], line[1][k])))
         if k:
@@ -333,17 +336,23 @@
             to_z.append((0, k, remote(sc.at[0, k], rc.at[0, k], line[0][k])))
         return same
 
+    def transposed(n):
+        at = slice(n * 128, (n + 1) * 128)
+        loads[4 + n].wait()
+        w_t[at] = jnp.transpose(w_v[:, at])
+
     pair = z // 2
+    transposed(2)
     forward(0)
     forward(1)
     forward_x(0)
+    transposed(0)
+    forward(2)
     forward_x(1)
-    forward(2)
-    for load in loads[4:]:
-        load.wait()
+    transposed(1)
+    forward(3)
     core_chunks(0)
     swap_near = project(pair)
-    forward(3)
     forward_x(2)
     forward_x(3)
     core_chunks(1)
@@ -358,14 +367,21 @@
     activate(1 - pair)
     core_far = to_core(1 - pair)
     gradients(0)
+    gradients(1)
     core_far.wait_recv()
     send_x(3)
     send_x(2)
-    send_z(1)
-    same = send_z(0)
-    gradients(1)
-    send_z(3)
-    send_z(2)
+    send_z(1, summed(1))
+    same = send_z(0, summed(0))
+    gradients(2)
+    mate_s[...] = summed(3).astype(BF16)
+    to_mate = remote(mate_s, mate_r, line[0][1])
+    far = summed(2)
+    gradients(3)
+    to_mate.wait_recv()
+    send_z(2, far + mate_r[...].astype(F32))
+    for n in (4, 5, 6):
+        gradients(n)
     total = [same, jnp.zeros_like(same)]
     for s_y, k, copy in to_z:
         copy.wait_recv()
@@ -380,18 +396,21 @@
         copy.wait_send()
 
 
-def output_kernel(slot_ref, sel_ref, gg_in, gu_in, gd_in, out_ref, tg_ref, gg_ref, gu_ref, gd_ref, rows, sems):
+def output_kernel(slot_ref, sel_ref, gg_in, gu_in, gd_in, out_ref, tg_ref, gg_ref, gu_ref, gd_ref, rows, held, sems):
     copies = []
 
     def move(src, dst):
         copy = pltpu.make_async_copy(src, dst, sems.at[len(copies)])
         copy.start()
         copies.append(copy)
+        return copy
 
     cut = gg_in.shape[0] // 2
+    arriving = []
     for n in range(2):
-        for src, dst in ((gg_in, gg_ref), (gu_in, gu_ref), (gd_in, gd_ref)):
-            move(src.at[pl.ds(n * cut, cut)], dst.at[pl.ds(n * cut, cut)])
+        at = pl.ds(n * cut, cut)
+        for i, (src, dst) in enumerate(((gg_in, gg_ref), (gu_in, gu_ref), (gd_in, gd_ref))):
+            arriving.append((move(src.at[at], held.at[i, at]), held.at[i, at], dst.at[at]))
     sel = sel_ref[...]
     low = row_ids(sel.shape) < 4
     slots = slot_ref[...].astype(BF16)
@@ -400,7 +419,10 @@
         picks = jnp.where(keep, sel, 0.0).astype(BF16)
         rows[n] = lax.dot_general(picks, slots, tn, preferred_element_type=F32).astype(BF16)
         move(rows.at[n], ref)
-    for copy in copies:
+        for copy, src, dst in arriving[3 * n : 3 * n + 3]:
+            copy.wait()
+            move(src, dst)
+    for copy in copies[6:]:
         copy.wait()
 
 
@@ -426,6 +448,7 @@
             pltpu.VMEM(gate_fixed.shape[::-1], jnp.int32),
             pltpu.VMEM((2 * n_tok, width), BF16),
             pltpu.VMEM((half, 384), BF16),
+            pltpu.VMEM((384, half), BF16),
             pieces(16, 2),
             chunks(16),
             pltpu.VMEM((16, 16, 384), BF16),
@@ -439,8 +462,10 @@
             pieces(2, 4),
             pieces(2, 4),
             pltpu.VMEM((16, half // 2), BF16),
+            pltpu.VMEM((16, half), BF16),
+            pltpu.VMEM((16, half), BF16),
             pltpu.VMEM((3, half, 128), F32),
-            pltpu.SemaphoreType.DMA((13,)),
+            pltpu.SemaphoreType.DMA((28,)),
             pltpu.SemaphoreType.DMA((copies,)),
             pltpu.SemaphoreType.DMA((copies,)),
         ],
@@ -456,7 +481,11 @@
         + (jax.ShapeDtypeStruct((half, 128), F32),) * 3,
         in_specs=[vmem, vmem, hbm, hbm, hbm],
         out_specs=(hbm,) * 5,
-        scratch_shapes=[pltpu.VMEM((2, n_tok, width), BF16), pltpu.SemaphoreType.DMA((8,))],
+        scratch_shapes=[
+            pltpu.VMEM((2, n_tok, width), BF16),
+            pltpu.VMEM((3, half, 128), F32),
+            pltpu.SemaphoreType.DMA((14,)),
+        ],
         compiler_params=pltpu.CompilerParams(vmem_limit_bytes=60 * 1024 * 1024),
         cost_estimate=pl.CostEstimate(flops=15_000_000, bytes_accessed=8_000_000, transcendentals=0),
         name="outputs",

time: 123 us -> 41.7 us (0.34)
  Pallas kernels: 122 us -> 40.8 us
    pallas_call x1, Pallas kernels: 85.5 us -> 4.14 us  [per_device_fused(): pl.pallas_call(output_kernel, out_shape=(jax.ShapeDtypeStruct((n_tok, wid...]
where the time goes in v4:
time: 41.7 us; the launch traced here: 41.5 us
  Pallas kernels  40.8 us (98%)
  between operations  0.64 us (2%)
    pallas_call x1, Pallas kernels, per_device_fused(): pl.pallas_call(exchange_kernel, out_shape=(*[jax.ShapeDtypeStruct((half,...  36.7 us
    pallas_call x1, Pallas kernels, per_device_fused(): pl.pallas_call(output_kernel, out_shape=(jax.ShapeDtypeStruct((n_tok, wid...  4.14 us

profile of v4, /device:TPU:0, one launch (start us, length us, event | category | flops | bytes accessed | tf_op | source)
XLA Modules:
  0.0 41.5 jit_solution(5354807444133208346)
XLA Ops:
  0.6 36.7 %exchange.1 = (f32[1792,128]{1,0:T(8,128)}, f32[1792,128]{1,0:T(8,128)}, f32[1792,128]{1,0:T(8,128)}, f32[8,3584]{1,0:T(8,128)}, f32[8,128]{1,0:T(8,128)}) custom-call(s32[8,128]{1,0:T(8,128)} %bitcast.11, s32[8,128]{1,0:T(8,128)} %bitcast.12, bf16[128,3584]{1,0:T(8,128)(2,1)} %tok_hbm.1, bf16[128,3584]{1,0:T(8,128)(2,1)} %cot_hbm.1, ...), custom_call_target="tpu_custom_call" | custom-call | flops 400000000 | bytes 6000000 | tf_op jit(solution)/shard_map/exchange/pallas_call | solution.py:437
  37.3 4.1 %outputs.1 = (bf16[128,3584]{1,0:T(8,128)(2,1)}, bf16[128,3584]{1,0:T(8,128)(2,1)}, f32[1792,128]{1,0:T(8,128)}, f32[1792,128]{1,0:T(8,128)}, f32[1792,128]{1,0:T(8,128)}) custom-call(f32[8,3584]{1,0:T(8,128)} %get-tuple-element.15.slot_ref, f32[8,128]{1,0:T(8,128)} %get-tuple-element.16.sel_ref, f32[1792,128]{1,0:T(8,128)} %get-tuple-element.17.gg_in, ...), custom_call_target="tpu_custom_call" | custom-call | flops 15000000 | bytes 8000000 | tf_op jit(solution)/shard_map/outputs/pallas_call | solution.py:478

commit v5 on v4

--- a/solution.py
+++ b/solution.py
@@ -136,9 +136,9 @@
 
 def exchange_kernel(
     ids_hbm, gates_hbm, tok_hbm, cot_hbm, wg_hbm, wu_hbm, wd_hbm,
-    gg_out, gu_out, gd_out, slot_out, sel_out,
+    x_out, act_out, slot_out, sel_out,
     ids_v, gates_v, both_v, w_v, w_t, gath, rows_v, act_v, part, pex_s, pex_r, res, ra, sb, rb, sc, rc,
-    across, mate_s, mate_r, grad_v, load_sem, send_sem, recv_sem,
+    across, mate_s, mate_r, load_sem, send_sem, recv_sem,
 ):
     y = lax.axis_index("dp")
     e = lax.axis_index("expert")
@@ -300,20 +300,6 @@
         sb[k] = core_sum(k, 1 - x).astype(BF16)
         to_x[k] = remote(sb.at[k], rb.at[k], peer_x)
 
-    grad_copies = []
-
-    def gradients(n):
-        cols = half // 7
-        rows = rows_v[:, :, n * cols : (n + 1) * cols].reshape(256, cols)
-        tn = (((0,), (0,)), ((), ()))
-        terms = lax.dot_general(rows, act_v[...].reshape(256, 384), tn, preferred_element_type=F32)
-        for i, out in enumerate((gg_out, gu_out, gd_out)):
-            at = pl.ds(n * cols, cols)
-            grad_v[i, at] = terms[:, i * 128 : (i + 1) * 128]
-            copy = pltpu.make_async_copy(grad_v.at[i, at], out.at[at], load_sem.at[7 + 3 * n + i])
-            copy.start()
-            grad_copies.append(copy)
-
     def summed(k):
         mid = core_sum(k, x)
         to_x[k].wait_recv()
@@ -357,6 +343,8 @@
     forward_x(3)
     core_chunks(1)
     swap_far = project(1 - pair)
+    keep_x = pltpu.make_async_copy(rows_v, x_out, load_sem.at[7])
+    keep_x.start()
     swap_near.wait_recv()
     activate(pair)
     core_near = to_core(pair)
@@ -366,22 +354,18 @@
     swap_far.wait_recv()
     activate(1 - pair)
     core_far = to_core(1 - pair)
-    gradients(0)
-    gradients(1)
+    keep_act = pltpu.make_async_copy(act_v, act_out, load_sem.at[8])
+    keep_act.start()
     core_far.wait_recv()
     send_x(3)
     send_x(2)
     send_z(1, summed(1))
     same = send_z(0, summed(0))
-    gradients(2)
     mate_s[...] = summed(3).astype(BF16)
     to_mate = remote(mate_s, mate_r, line[0][1])
     far = summed(2)
-    gradients(3)
     to_mate.wait_recv()
     send_z(2, far + mate_r[...].astype(F32))
-    for n in (4, 5, 6):
-        gradients(n)
     total = [same, jnp.zeros_like(same)]
     for s_y, k, copy in to_z:
         copy.wait_recv()
@@ -390,40 +374,23 @@
     scale = jnp.where(row_ids((8, 1)) < 4, gate8, 1.0)
     slot_out[:, :half] = jnp.where(y == 0, mine8, got8) * scale
     slot_out[:, half:] = jnp.where(y == 0, got8, mine8) * scale
-    for copy in grad_copies:
-        copy.wait()
+    keep_x.wait()
+    keep_act.wait()
     for copy in started:
         copy.wait_send()
 
 
-def output_kernel(slot_ref, sel_ref, gg_in, gu_in, gd_in, out_ref, tg_ref, gg_ref, gu_ref, gd_ref, rows, held, sems):
-    copies = []
-
-    def move(src, dst):
-        copy = pltpu.make_async_copy(src, dst, sems.at[len(copies)])
-        copy.start()
-        copies.append(copy)
-        return copy
-
-    cut = gg_in.shape[0] // 2
-    arriving = []
-    for n in range(2):
-        at = pl.ds(n * cut, cut)
-        for i, (src, dst) in enumerate(((gg_in, gg_ref), (gu_in, gu_ref), (gd_in, gd_ref))):
-            arriving.append((move(src.at[at], held.at[i, at]), held.at[i, at], dst.at[at]))
+def output_kernel(x_ref, act_ref, slot_ref, sel_ref, out_ref, tg_ref, gg_ref, gu_ref, gd_ref):
     sel = sel_ref[...]
     low = row_ids(sel.shape) < 4
     slots = slot_ref[...].astype(BF16)
     tn = (((0,), (0,)), ((), ()))
-    for n, (ref, keep) in enumerate(((out_ref, low), (tg_ref, jnp.logical_not(low)))):
+    for ref, keep in ((out_ref, low), (tg_ref, jnp.logical_not(low))):
         picks = jnp.where(keep, sel, 0.0).astype(BF16)
-        rows[n] = lax.dot_general(picks, slots, tn, preferred_element_type=F32).astype(BF16)
-        move(rows.at[n], ref)
-        for copy, src, dst in arriving[3 * n : 3 * n + 3]:
-            copy.wait()
-            move(src, dst)
-    for copy in copies[6:]:
-        copy.wait()
+        ref[...] = lax.dot_general(picks, slots, tn, preferred_element_type=F32).astype(BF16)
+    grads = lax.dot_general(x_ref[...], act_ref[...], tn, preferred_element_type=F32)
+    for n, ref in enumerate((gg_ref, gu_ref, gd_ref)):
+        ref[...] = grads[:, n * 128 : (n + 1) * 128]
 
 
 def per_device_fused(tokens, out_cotangent, expert_ids, gate_fixed, w_gate, w_up, w_down):
@@ -434,15 +401,16 @@
     copies = 35
     chunks = lambda n: pltpu.VMEM((n, 16, half), BF16)
     pieces = lambda m, n: pltpu.VMEM((m, n, 16, half // 2), BF16)
-    gg, gu, gd, slots, sel = pl.pallas_call(
+    x_all, act, slots, sel = pl.pallas_call(
         exchange_kernel,
         out_shape=(
-            *[jax.ShapeDtypeStruct((half, 128), F32)] * 3,
-            jax.ShapeDtypeStruct((8, width), F32),
-            jax.ShapeDtypeStruct((8, n_tok), F32),
+            pltpu.VMEM((16, 16, half), BF16),
+            pltpu.VMEM((16, 16, 384), BF16),
+            pltpu.VMEM((8, width), F32),
+            pltpu.VMEM((8, n_tok), F32),
         ),
         in_specs=[hbm] * 7,
-        out_specs=(hbm, hbm, hbm, vmem, vmem),
+        out_specs=(vmem,) * 4,
         scratch_shapes=[
             pltpu.VMEM(expert_ids.shape[::-1], jnp.int32),
             pltpu.VMEM(gate_fixed.shape[::-1], jnp.int32),
@@ -464,8 +432,7 @@
             pltpu.VMEM((16, half // 2), BF16),
             pltpu.VMEM((16, half), BF16),
             pltpu.VMEM((16, half), BF16),
-            pltpu.VMEM((3, half, 128), F32),
-            pltpu.SemaphoreType.DMA((28,)),
+            pltpu.SemaphoreType.DMA((9,)),
             pltpu.SemaphoreType.DMA((copies,)),
             pltpu.SemaphoreType.DMA((copies,)),
         ],
@@ -475,21 +442,25 @@
         cost_estimate=pl.CostEstimate(flops=400_000_000, bytes_accessed=6_000_000, transcendentals=16384),
         name="exchange",
     )(expert_ids.T, gate_fixed.T, tokens, out_cotangent, w_gate[0], w_up[0], w_down[0])
+    steps = 2
+    grad_spec = pl.BlockSpec((half // steps, 128), lambda i: (i, 0))
+    tok_spec = pl.BlockSpec((n_tok, width // steps), lambda i: (0, i))
     layer_out, token_grad, gg, gu, gd = pl.pallas_call(
         output_kernel,
+        grid=(steps,),
         out_shape=(jax.ShapeDtypeStruct((n_tok, width), BF16),) * 2
         + (jax.ShapeDtypeStruct((half, 128), F32),) * 3,
-        in_specs=[vmem, vmem, hbm, hbm, hbm],
-        out_specs=(hbm,) * 5,
-        scratch_shapes=[
-            pltpu.VMEM((2, n_tok, width), BF16),
-            pltpu.VMEM((3, half, 128), F32),
-            pltpu.SemaphoreType.DMA((14,)),
+        in_specs=[
+            pl.BlockSpec((256, half // steps), lambda i: (0, i)),
+            pl.BlockSpec((256, 384), lambda i: (0, 0)),
+            pl.BlockSpec((8, width // steps), lambda i: (0, i)),
+            pl.BlockSpec((8, n_tok), lambda i: (0, 0)),
         ],
-        compiler_params=pltpu.CompilerParams(vmem_limit_bytes=60 * 1024 * 1024),
-        cost_estimate=pl.CostEstimate(flops=15_000_000, bytes_accessed=8_000_000, transcendentals=0),
+        out_specs=(tok_spec, tok_spec, grad_spec, grad_spec, grad_spec),
+        compiler_params=pltpu.CompilerParams(vmem_limit_bytes=32 * 1024 * 1024),
+        cost_estimate=pl.CostEstimate(flops=400_000_000, bytes_accessed=6_000_000, transcendentals=0),
         name="outputs",
-    )(slots, sel, gg, gu, gd)
+    )(x_all.reshape(256, half), act.reshape(256, 384), slots, sel)
     return (layer_out, token_grad, gg[None], gu[None], gd[None])
 
 

time: 41.7 us -> 39.4 us (0.945)
  Pallas kernels: 40.8 us -> 38.5 us
    pallas_call x2, Pallas kernels: 40.8 us -> 38.5 us  [the longest x1 35.9 us: per_device_fused(): pl.pallas_call(exchange_kernel, out_shape=(pltpu.VMEM((16, 16, half), BF1...]
where the time goes in v5:
time: 39.4 us; the launch traced here: 39.2 us
  Pallas kernels  38.5 us (98%)
  between operations  0.64 us (2%)
    pallas_call x1, Pallas kernels, per_device_fused(): pl.pallas_call(exchange_kernel, out_shape=(pltpu.VMEM((16, 16, half), BF1...  35.9 us
    pallas_call x1, Pallas kernels, per_device_fused(): pl.pallas_call(output_kernel, grid=(steps,), out_shape=(jax.ShapeDtypeStr...  2.67 us

profile of v5, /device:TPU:0, one launch (start us, length us, event | category | flops | bytes accessed | tf_op | source)
XLA Modules:
  0.0 39.2 jit_solution(3794215695305498028)
XLA Ops:
  0.6 35.9 %exchange.1 = (bf16[16,16,1792]{2,1,0:T(8,128)(2,1)S(1)}, bf16[16,16,384]{2,1,0:T(8,128)(2,1)S(1)}, f32[8,3584]{1,0:T(8,128)S(1)}, f32[8,128]{1,0:T(8,128)S(1)}) custom-call(s32[8,128]{1,0:T(8,128)} %bitcast.15, s32[8,128]{1,0:T(8,128)} %bitcast.16, bf16[128,3584]{1,0:T(8,128)(2,1)} %tok_hbm.1, bf16[128,3584]{1,0:T(8,128)(2,1)} %cot_hbm.1, ...), custom_call_target="tpu_custom_call" | custom-call | flops 400000000 | bytes 6000000 | tf_op jit(solution)/shard_map/exchange/pallas_call | solution.py:404
  36.5 2.7 %outputs.1 = (bf16[128,3584]{1,0:T(8,128)(2,1)}, bf16[128,3584]{1,0:T(8,128)(2,1)}, f32[1792,128]{1,0:T(8,128)}, f32[1792,128]{1,0:T(8,128)}, f32[1792,128]{1,0:T(8,128)}) custom-call(bf16[256,1792]{1,0:T(8,128)(2,1)S(1)} %bitcast.10, bf16[256,384]{1,0:T(8,128)(2,1)S(1)} %bitcast.11, f32[8,3584]{1,0:T(8,128)S(1)} %get-tuple-element.16.slot_ref, ...), custom_call_target="tpu_custom_call" | custom-call | flops 400000000 | bytes 6000000 | tf_op jit(solution)/shard_map/outputs/pallas_call | solution.py:448

commit v6 on v2

--- a/solution.py
+++ b/solution.py
@@ -137,7 +137,7 @@
 def exchange_kernel(
     ids_hbm, gates_hbm, tok_hbm, cot_hbm, wg_hbm, wu_hbm, wd_hbm,
     x_out, act_out, slot_out, sel_out,
-    ids_v, gates_v, both_v, w_v, gath, rows_v, act_v, part, pex_s, pex_r, res, ra, sb, rb, sc, rc,
+    ids_v, gates_v, both_v, w_v, w_t, gath, rows_v, act_v, part, pex_s, pex_r, res, ra, sb, rb, sc, rc,
     across, load_sem, send_sem, recv_sem,
 ):
     y = lax.axis_index("dp")
@@ -263,9 +263,8 @@
         d_gate = (d_hidden * up_pre * sig * (1.0 + gate_pre * (1.0 - sig))).astype(BF16)
         d_up = (d_hidden * act).astype(BF16)
         d_both = jnp.concatenate([d_gate, d_up], axis=1)
-        nt = (((1,), (1,)), ((), ()))
-        out = lax.dot_general(hidden, w_v[:, 256:], nt, preferred_element_type=F32)
-        grad = lax.dot_general(d_both, w_v[:, :256], nt, preferred_element_type=F32)
+        out = jnp.dot(hidden, w_t[256:], preferred_element_type=F32)
+        grad = jnp.dot(d_both, w_t[:256], preferred_element_type=F32)
         res[pl.ds(h * 8, 8)] = jnp.concatenate(
             [out.reshape(8, 8, half), grad.reshape(8, 8, half)], axis=1
         ).astype(BF16)
@@ -288,6 +287,8 @@
     swap_other = project(1 - c)
     keep_x = pltpu.make_async_copy(rows_v, x_out, load_sem.at[7])
     keep_x.start()
+    for n in (0, 128, 256):
+        w_t[n : n + 128] = jnp.transpose(w_v[:, n : n + 128])
     swap_other.wait_recv()
     activate(1 - c)
     to_core = []
@@ -362,18 +363,19 @@
     x_all, act, slots, sel = pl.pallas_call(
         exchange_kernel,
         out_shape=(
-            jax.ShapeDtypeStruct((16, 16, half), BF16),
-            jax.ShapeDtypeStruct((16, 16, 384), BF16),
-            jax.ShapeDtypeStruct((8, width), F32),
-            jax.ShapeDtypeStruct((8, n_tok), F32),
+            pltpu.VMEM((16, 16, half), BF16),
+            pltpu.VMEM((16, 16, 384), BF16),
+            pltpu.VMEM((8, width), F32),
+            pltpu.VMEM((8, n_tok), F32),
         ),
         in_specs=[hbm] * 7,
-        out_specs=(hbm, hbm, vmem, vmem),
+        out_specs=(vmem,) * 4,
         scratch_shapes=[
             pltpu.VMEM(expert_ids.shape[::-1], jnp.int32),
             pltpu.VMEM(gate_fixed.shape[::-1], jnp.int32),
             pltpu.VMEM((2 * n_tok, width), BF16),
             pltpu.VMEM((half, 384), BF16),
+            pltpu.VMEM((384, half), BF16),
             pieces(16, 2),
             chunks(16),
             pltpu.VMEM((16, 16, 384), BF16),
@@ -412,7 +414,7 @@
             pl.BlockSpec((8, n_tok), lambda i: (0, 0)),
         ],
         out_specs=(tok_spec, tok_spec, grad_spec, grad_spec, grad_spec),
-        compiler_params=pltpu.CompilerParams(vmem_limit_bytes=60 * 1024 * 1024),
+        compiler_params=pltpu.CompilerParams(vmem_limit_bytes=32 * 1024 * 1024),
         cost_estimate=pl.CostEstimate(flops=400_000_000, bytes_accessed=6_000_000, transcendentals=0),
         name="outputs",
     )(x_all.reshape(256, half), act.reshape(256, 384), slots, sel)

time: 38.3 us -> 36.5 us (0.953)
  Pallas kernels: 37.5 us -> 35.7 us
    pallas_call x1, Pallas kernels: 3.61 us -> 2.67 us  [per_device_fused(): pl.pallas_call(output_kernel, grid=(steps,), out_shape=(jax.ShapeDtypeStr...]
    pallas_call x1, Pallas kernels: 33.9 us -> 33 us  [per_device_fused(): pl.pallas_call(exchange_kernel, out_shape=(pltpu.VMEM((16, 16, half), BF1...]
where the time goes in v6:
time: 36.5 us; the launch traced here: 36.3 us
  Pallas kernels  35.7 us (98%)
  between operations  0.64 us (2%)
    pallas_call x1, Pallas kernels, per_device_fused(): pl.pallas_call(exchange_kernel, out_shape=(pltpu.VMEM((16, 16, half), BF1...  33 us
    pallas_call x1, Pallas kernels, per_device_fused(): pl.pallas_call(output_kernel, grid=(steps,), out_shape=(jax.ShapeDtypeStr...  2.67 us

profile of v6, /device:TPU:0, one launch (start us, length us, event | category | flops | bytes accessed | tf_op | source)
XLA Modules:
  0.0 36.3 jit_solution(16137270184598602921)
XLA Ops:
  0.6 33.0 %exchange.1 = (bf16[16,16,1792]{2,1,0:T(8,128)(2,1)S(1)}, bf16[16,16,384]{2,1,0:T(8,128)(2,1)S(1)}, f32[8,3584]{1,0:T(8,128)S(1)}, f32[8,128]{1,0:T(8,128)S(1)}) custom-call(s32[8,128]{1,0:T(8,128)} %bitcast.15, s32[8,128]{1,0:T(8,128)} %bitcast.16, bf16[128,3584]{1,0:T(8,128)(2,1)} %tok_hbm.1, bf16[128,3584]{1,0:T(8,128)(2,1)} %cot_hbm.1, ...), custom_call_target="tpu_custom_call" | custom-call | flops 400000000 | bytes 6000000 | tf_op jit(solution)/shard_map/exchange/pallas_call | solution.py:363
  33.7 2.7 %outputs.1 = (bf16[128,3584]{1,0:T(8,128)(2,1)}, bf16[128,3584]{1,0:T(8,128)(2,1)}, f32[1792,128]{1,0:T(8,128)}, f32[1792,128]{1,0:T(8,128)}, f32[1792,128]{1,0:T(8,128)}) custom-call(bf16[256,1792]{1,0:T(8,128)(2,1)S(1)} %bitcast.10, bf16[256,384]{1,0:T(8,128)(2,1)S(1)} %bitcast.11, f32[8,3584]{1,0:T(8,128)S(1)} %get-tuple-element.16.slot_ref, ...), custom_call_target="tpu_custom_call" | custom-call | flops 400000000 | bytes 6000000 | tf_op jit(solution)/shard_map/outputs/pallas_call | solution.py:405
